TPU v7x, 128 devices: a whole 4x4x4 slice. The times are simulated.
128 devices in a mesh: dp: 16 (over x, z_lo, core), ctx: 8 (over y, z_hi).
Axes of the slice: x: 4, y: 4, z: 4 (z_hi: 2, z_lo: 2; z = z_hi * 2 + z_lo), core: 2. Of those that a mesh axis runs over, the one named last changes fastest.
Arguments:
- queries: bfloat16 [16, 1024, 2048], P('dp', 'ctx'), may hold values from -8 to 8
- keys: bfloat16 [16, 1024, 128], P('dp', 'ctx'), may hold values from -8 to 8
- values: bfloat16 [16, 1024, 128], P('dp', 'ctx'), may hold values from -24 to 24
- expert_ids: int32 [16, 1024, 8], P('dp', 'ctx'), may hold values from 0 to 127, all different within a row; in each aligned block of 128 rows (0 to 127, 128 to 255, ..., all dimensions but the last counted through in order) at most 10 rows name the same one
- router_scores: float32 [16, 1024, 8], P('dp', 'ctx'), may hold values from 0.25 to 5
- gate_weight: bfloat16 [128, 2048, 768], P(('dp', 'ctx')), may hold values from -0.125 to 0.125
- up_weight: bfloat16 [128, 2048, 768], P(('dp', 'ctx')), may hold values from -0.125 to 0.125
- down_weight: bfloat16 [128, 768, 2048], P(('dp', 'ctx')), may hold values from -0.21875 to 0.21875
- out_grad: bfloat16 [16, 1024, 2048], P('dp', 'ctx'), may hold values from -6 to 6
Outputs:
- moe_out: bfloat16 [16, 1024, 2048], P('dp', 'ctx')
- query_grad: bfloat16 [16, 1024, 2048], P('dp', 'ctx')
- key_grad: bfloat16 [16, 1024, 128], P('dp', 'ctx')
- value_grad: bfloat16 [16, 1024, 128], P('dp', 'ctx')
- score_grad: float32 [16, 1024, 8], P('dp', 'ctx')
Inputs may be any that keep to these rules, and one draw needn't show every extreme that they name: `expert_ids`: the 8 experts of a token are distinct. Among the 128 tokens of one device no expert is picked more than 10 times, and in every draw some expert is picked exactly 10 times by some device's tokens.
All inputs are finite; a program needn't handle non-finite values.
Results may differ from a plain program's by a relative error of at most 0.038.
Values may be sent and summed in bfloat16 or wider, within the bound.
A program may use at most 192 MiB of HBM per device.

v0:
```python
import jax
import jax.numpy as jnp
from jax import lax
from jax.sharding import PartitionSpec as P

KVH = 2
HD = 64
GROUP = 16
TOPK = 8


EPSILON = 1e-06
NEGATIVE = -1e30


def shards(
    queries, keys, values, expert_ids, router_scores, gate_weight, up_weight, down_weight, out_grad
):
    rows_here = queries.shape[1]
    model_width = queries.shape[2]
    pair_width = keys.shape[2]
    score_scale = HD ** (-0.5)
    local_queries = queries[0]
    query_pos = lax.axis_index("ctx") * rows_here + jnp.arange(rows_here, dtype=jnp.int32)
    query_sets = [
        local_queries[:, head_set * GROUP * HD : (head_set + 1) * GROUP * HD].reshape(
            rows_here, GROUP, HD
        )
        for head_set in range(KVH)
    ]
    running_max = jnp.full((GROUP * KVH, rows_here), NEGATIVE, jnp.float32)
    weighted = jnp.zeros((rows_here, model_width), jnp.float32)
    block_keys = lax.all_gather(keys, "ctx", axis=1, tiled=True)[0]
    block_values = lax.all_gather(values, "ctx", axis=1, tiled=True)[0]
    block_rows = block_keys.shape[0]
    key_pos = jnp.arange(block_rows, dtype=jnp.int32)
    allowed = (key_pos[None, :] <= query_pos[:, None])[None]
    new_maxes = []
    new_sums = []
    new_weighted = []
    for fold_head_set in range(KVH):
        fold_head_cols = slice(fold_head_set * HD, (fold_head_set + 1) * HD)
        fold_scores = (
            jnp.einsum(
                "thd,sd->hts",
                query_sets[fold_head_set],
                block_keys[:, fold_head_cols],
                preferred_element_type=jnp.float32,
            )
            * score_scale
        )
        fold_scores = jnp.where(allowed, fold_scores, NEGATIVE)
        old_max = running_max[fold_head_set * GROUP : (fold_head_set + 1) * GROUP]
        new_max = jnp.maximum(old_max, jnp.max(fold_scores, axis=2))
        exp_scores = jnp.where(allowed, jnp.exp(fold_scores - new_max[:, :, None]), 0.0)
        shrink = jnp.exp(old_max - new_max)
        new_maxes.append(new_max)
        new_sums.append(jnp.sum(exp_scores, axis=2))
        update = jnp.einsum(
            "hts,sd->thd",
            exp_scores.astype(jnp.bfloat16),
            block_values[:, fold_head_cols],
            preferred_element_type=jnp.float32,
        )
        previous = weighted[
            :, fold_head_set * GROUP * HD : (fold_head_set + 1) * GROUP * HD
        ].reshape(rows_here, GROUP, HD)
        new_weighted.append(
            (previous * shrink.T[:, :, None] + update).reshape(rows_here, GROUP * HD)
        )
    running_max = jnp.concatenate(new_maxes)
    running_sum = jnp.concatenate(new_sums)
    weighted = jnp.concatenate(new_weighted, axis=1)
    all_keys, all_values = (
        lax.all_gather(keys, "ctx", axis=1, tiled=True),
        lax.all_gather(values, "ctx", axis=1, tiled=True),
    )
    attn_out = (
        (weighted.reshape(rows_here, GROUP * KVH, HD) / running_sum.T[:, :, None])
        .reshape(rows_here, model_width)
        .astype(jnp.bfloat16)
    )
    log_total = running_max + jnp.log(running_sum)
    attn_wide = attn_out.astype(jnp.float32)
    inv_rms = lax.rsqrt(jnp.mean(attn_wide * attn_wide, axis=1, keepdims=True) + EPSILON)
    normed = (attn_wide * inv_rms).astype(jnp.bfloat16)
    dp_count = lax.axis_size("dp")
    ctx_count = lax.axis_size("ctx")
    experts = dp_count * ctx_count
    capacity = 10 * rows_here * TOPK // (8 * experts)
    expert_picks = expert_ids[0].reshape(-1)
    pick_count = expert_picks.shape[0]
    onehot = (expert_picks[:, None] == jnp.arange(experts, dtype=jnp.int32)[None, :]).astype(
        jnp.int32
    )
    slot_index = jnp.sum(jnp.cumsum(onehot, axis=0) * onehot, axis=1) - 1
    placed = expert_picks * capacity + slot_index
    slot_pick = (
        jnp.full((experts * capacity,), pick_count, jnp.int32)
        .at[placed]
        .set(jnp.arange(pick_count, dtype=jnp.int32))
    )
    slot_token = slot_pick // TOPK
    normed_pad = jnp.concatenate([normed, jnp.zeros((1, model_width), jnp.bfloat16)])
    outgoing = normed_pad[slot_token].reshape(experts, capacity, model_width)
    w_gate = gate_weight[0]
    w_up = up_weight[0]
    w_down = down_weight[0]
    arrived_rows = lax.all_to_all(outgoing, ("dp", "ctx"), split_axis=0, concat_axis=0, tiled=True)
    sources = arrived_rows.shape[0]
    slots = arrived_rows.shape[1]
    flat_rows = arrived_rows.reshape(sources * slots, model_width)
    expert_gate_act = jnp.dot(flat_rows, w_gate, preferred_element_type=jnp.float32)
    expert_up_act = jnp.dot(flat_rows, w_up, preferred_element_type=jnp.float32)
    hidden = (expert_gate_act * jax.nn.sigmoid(expert_gate_act) * expert_up_act).astype(
        jnp.bfloat16
    )
    produced = jnp.dot(hidden, w_down, preferred_element_type=jnp.float32).astype(jnp.bfloat16)
    produced, gate_act, up_act = (
        produced.reshape(sources, slots, model_width),
        expert_gate_act.reshape(sources, slots, -1),
        expert_up_act.reshape(sources, slots, -1),
    )
    returned = lax.all_to_all(produced, ("dp", "ctx"), split_axis=0, concat_axis=0, tiled=True)
    pick_out = returned.reshape(experts * capacity, model_width)[placed].reshape(
        rows_here, TOPK, model_width
    )
    raw_scores = router_scores[0]
    score_total = jnp.sum(raw_scores, axis=1, keepdims=True)
    mixing = raw_scores / score_total
    mixed = jnp.sum(mixing[:, :, None] * pick_out.astype(jnp.float32), axis=1)
    moe_out = mixed.astype(jnp.bfloat16)[None]
    grad_rows = out_grad[0]
    weight_grad = jnp.einsum("td,tkd->tk", grad_rows, pick_out, preferred_element_type=jnp.float32)
    score_grad = (weight_grad - jnp.sum(mixing * weight_grad, axis=1, keepdims=True)) / score_total
    mixing_pad = jnp.concatenate([mixing.reshape(-1), jnp.zeros((1,), jnp.float32)])
    grad_pad = jnp.concatenate([grad_rows, jnp.zeros((1, model_width), jnp.bfloat16)])
    grad_sent = (
        (mixing_pad[slot_pick][:, None] * grad_pad[slot_token].astype(jnp.float32))
        .astype(jnp.bfloat16)
        .reshape(experts, capacity, model_width)
    )
    arrived_grad = lax.all_to_all(grad_sent, ("dp", "ctx"), split_axis=0, concat_axis=0, tiled=True)
    flat_grad = arrived_grad.reshape(-1, model_width)
    gate_flat = gate_act.reshape(flat_grad.shape[0], -1)
    up_flat = up_act.reshape(flat_grad.shape[0], -1)
    hidden_grad = jnp.dot(flat_grad, w_down.T, preferred_element_type=jnp.float32)
    sigmoid_gate = jax.nn.sigmoid(gate_flat)
    gate_grad = (
        hidden_grad * up_flat * sigmoid_gate * (1.0 + gate_flat * (1.0 - sigmoid_gate))
    ).astype(jnp.bfloat16)
    up_grad = (hidden_grad * gate_flat * sigmoid_gate).astype(jnp.bfloat16)
    row_grad = jnp.dot(gate_grad, w_gate.T, preferred_element_type=jnp.float32) + jnp.dot(
        up_grad, w_up.T, preferred_element_type=jnp.float32
    )
    returned_grad = lax.all_to_all(
        row_grad.astype(jnp.bfloat16).reshape(arrived_grad.shape),
        ("dp", "ctx"),
        split_axis=0,
        concat_axis=0,
        tiled=True,
    )
    normed_grad = jnp.sum(
        returned_grad.reshape(experts * capacity, model_width)[placed]
        .reshape(rows_here, TOPK, model_width)
        .astype(jnp.float32),
        axis=1,
    )
    attn_grad = (
        inv_rms * normed_grad
        - inv_rms**3 * attn_wide * jnp.mean(normed_grad * attn_wide, axis=1, keepdims=True)
    ).astype(jnp.bfloat16)
    full_keys = all_keys[0]
    full_values = all_values[0]
    full_pos = jnp.arange(full_keys.shape[0], dtype=jnp.int32)
    allowed_full = (full_pos[None, :] <= query_pos[:, None])[None]
    query_parts, score_sets, weight_sets, grad_sets = ([], [], [], [])
    for head_set in range(KVH):
        head_cols = slice(head_set * HD, (head_set + 1) * HD)
        group_cols = slice(head_set * GROUP * HD, (head_set + 1) * GROUP * HD)
        key_set = full_keys[:, head_cols]
        scores = (
            jnp.einsum(
                "thd,sd->hts", query_sets[head_set], key_set, preferred_element_type=jnp.float32
            )
            * score_scale
        )
        soft_weights = jnp.where(
            allowed_full,
            jnp.exp(scores - log_total[head_set * GROUP : (head_set + 1) * GROUP][:, :, None]),
            0.0,
        )
        grad_set = attn_grad[:, group_cols].reshape(rows_here, GROUP, HD)
        out_set = attn_out[:, group_cols].reshape(rows_here, GROUP, HD)
        row_delta = jnp.sum(grad_set.astype(jnp.float32) * out_set.astype(jnp.float32), axis=2).T
        prob_grad = jnp.einsum(
            "thd,sd->hts", grad_set, full_values[:, head_cols], preferred_element_type=jnp.float32
        )
        score_grads = (soft_weights * (prob_grad - row_delta[:, :, None]) * score_scale).astype(
            jnp.bfloat16
        )
        query_parts.append(
            jnp.einsum(
                "hts,sd->thd", score_grads, key_set, preferred_element_type=jnp.float32
            ).reshape(rows_here, GROUP * HD)
        )
        score_sets.append(score_grads)
        weight_sets.append(soft_weights.astype(jnp.bfloat16))
        grad_sets.append(grad_set)
    query_grad = jnp.concatenate(query_parts, axis=1).astype(jnp.bfloat16)[None]
    key_parts = []
    value_parts = []
    for head_set in range(KVH):
        score_slice = score_sets[head_set]
        weight_slice = weight_sets[head_set]
        key_parts.append(
            jnp.einsum(
                "hts,thd->sd", score_slice, query_sets[head_set], preferred_element_type=jnp.float32
            )
        )
        value_parts.append(
            jnp.einsum(
                "hts,thd->sd", weight_slice, grad_sets[head_set], preferred_element_type=jnp.float32
            )
        )
    pair_grad = lax.psum_scatter(
        jnp.concatenate(key_parts + value_parts, axis=1), "ctx", scatter_dimension=0, tiled=True
    )
    key_grad = pair_grad[:, :pair_width].astype(jnp.bfloat16)[None]
    value_grad = pair_grad[:, pair_width:].astype(jnp.bfloat16)[None]
    return (moe_out, query_grad, key_grad, value_grad, score_grad[None])


def solution(mesh):
    placed = (
        P("dp", "ctx", None),
        P("dp", "ctx", None),
        P("dp", "ctx", None),
        P("dp", "ctx", None),
        P("dp", "ctx", None),
        P(("dp", "ctx"), None, None),
        P(("dp", "ctx"), None, None),
        P(("dp", "ctx"), None, None),
        P("dp", "ctx", None),
    )
    return jax.shard_map(
        shards,
        mesh=mesh,
        in_specs=placed,
        out_specs=(
            P("dp", "ctx", None),
            P("dp", "ctx", None),
            P("dp", "ctx", None),
            P("dp", "ctx", None),
            P("dp", "ctx", None),
        ),
        check_vma=False,
    )
```

profile of v0, /device:TPU:0, one launch (start us, length us, event | category | flops | bytes accessed | tf_op | source)
XLA Modules:
  0.0 706.4 jit_solution(7292582317001054523)
XLA Ops:
  7.2 0.9 copy.45
  8.3 1.3 broadcast_multiply_fusion
  9.7 0.9 copy.37
  10.6 32.3 %all_gather.8 = bf16[1,1024,128]{1,2,0:T(8,128)(2,1)} all-gather(bf16[1,128,128]{1,2,0:T(8,128)(2,1)S(1)} %copy.37), channel_id=1, replica_groups=mesh['dp'=16,'ctx'=8] {'ctx'}, dimensions={1}, use_global_device_ids=true | all-gather | bytes 294912 | tf_op jit(solution)/shard_map/all_gather | solution.py:33
  42.9 1.9 fusion.102
  44.7 1.1 copy.38
  45.8 5.5 fusion.10
  52.0 1.8 copy.41
  53.8 10.6 %fusion.14 = (f32[16,128]{1,0:T(8,128)}, f32[16,128]{1,0:T(8,128)S(1)}, f32[1024,128,16]{1,0,2:T(8,128)}) fusion(f32[1024,128,16]{1,0,2:T(8,128)} %get-tuple-element.42, f32[16,128]{1,0:T(8,128)S(1)} %get-tuple-element.36, pred[128,1024]{0,1:T(8,128)(4,1)S(1)} %iota_compare_fusion.2, bf16[128,16,64]{0,2,1:T(8,128)(2,1)} %bitcast.220, ...), kind=kOutput, calls=%fused_computation.33 | convolution fusion | flops 285208576 | bytes 17326080 | tf_op jit(solution)/shard_map/thd,sd->hts/dot_general | solution.py:44
  65.3 30.4 %all_gather.9 = bf16[1,1024,128]{1,2,0:T(8,128)(2,1)S(1)} all-gather(bf16[1,128,128]{1,2,0:T(8,128)(2,1)S(1)} %copy.39), channel_id=1, replica_groups=mesh['dp'=16,'ctx'=8] {'ctx'}, dimensions={1}, use_global_device_ids=true | all-gather | bytes 294912 | tf_op jit(solution)/shard_map/all_gather | solution.py:34
  95.7 4.6 fusion.16
  100.4 2.0 fusion.51
  102.6 2.0 fusion.54
  104.6 1.0 multiply_reduce_fusion.1
  105.6 2.0 copy.43
  109.3 1.1 broadcast_add_fusion
  111.1 4.3 scatter_custom_fusion
  115.5 1.2 fusion.63
  117.6 11.9 %gather_fusion = bf16[1280,2048]{1,0:T(8,128)(2,1)} fusion(bf16[129,2048]{1,0:T(8,128)(2,1)} %concatenate.39, s32[2048]{0:T(1024)S(1)} %get-tuple-element.45), kind=kCustom, calls=%fused_computation | custom fusion | bytes 10490880 | tf_op jit(solution)/shard_map/gather | solution.py:105
  129.5 9.5 %reshape.257 = bf16[128,10,2048]{2,1,0:T(8,128)(2,1)} reshape(bf16[1280,2048]{1,0:T(8,128)(2,1)} %gather_fusion) | data formatting | bytes 10485760 | tf_op jit(solution)/shard_map/reshape | solution.py:105
  139.1 9.4 %all-to-all-start = ((bf16[128,10,2048]{2,1,0:T(8,128)(2,1)}), bf16[128,10,2048]{2,1,0:T(8,128)(2,1)}, u32[]{:S(2)}, u32[]{:S(2)}) async-start(bf16[128,10,2048]{2,1,0:T(8,128)(2,1)} %reshape.257), calls=%async_computation | async-start | bytes 16777216 | tf_op jit(solution)/shard_map/all_to_all | solution.py:109
  149.4 7.1 %gather_fusion.2 = f32[1280]{0:T(1024)S(1)} fusion(f32[1025]{0:T(1024)S(1)} %pad_maximum_fusion.3, s32[2048]{0:T(1024)S(1)} %get-tuple-element.44), kind=kCustom, calls=%fused_computation.2 | custom fusion | bytes 15360 | tf_op jit(solution)/shard_map/gather | solution.py:139
  156.7 1.9 concatenate.42
  158.6 11.9 %gather_fusion.3 = bf16[1280,2048]{1,0:T(8,128)(2,1)} fusion(bf16[129,2048]{1,0:T(8,128)(2,1)} %concatenate.42, s32[2048]{0:T(1024)S(1)} %get-tuple-element.45), kind=kCustom, calls=%fused_computation.3 | custom fusion | bytes 10490880 | tf_op jit(solution)/shard_map/gather | solution.py:139
  170.5 10.3 %reshape.267 = f32[128,10,2048]{2,1,0:T(8,128)} reshape(bf16[1280,2048]{1,0:T(8,128)(2,1)} %gather_fusion.3) | data formatting | bytes 15728640 | tf_op jit(solution)/shard_map/convert_element_type | solution.py:139
  180.8 9.0 %multiply_convert_fusion = bf16[128,10,2048]{2,1,0:T(8,128)(2,1)} fusion(f32[128,10,2048]{2,1,0:T(8,128)} %reshape.267, f32[128,10]{1,0:T(8,128)S(1)} %mul.169), kind=kLoop, calls=%fused_computation.6 | loop fusion | flops 5242880 | bytes 15733760 | tf_op jit(solution)/shard_map/convert_element_type | solution.py:140
  189.9 61.2 %all-to-all-done = bf16[128,10,2048]{2,1,0:T(8,128)(2,1)} async-done(((bf16[128,10,2048]{2,1,0:T(8,128)(2,1)}), bf16[128,10,2048]{2,1,0:T(8,128)(2,1)}, u32[]{:S(2)}, u32[]{:S(2)}) %all-to-all-start) | async-done | bytes 5242912 | tf_op jit(solution)/shard_map/all_to_all | solution.py:109
  251.1 12.4 %all-to-all-start.2 = ((bf16[128,10,2048]{2,1,0:T(8,128)(2,1)}), bf16[128,10,2048]{2,1,0:T(8,128)(2,1)}, u32[]{:S(2)}, u32[]{:S(2)}) async-start(bf16[128,10,2048]{2,1,0:T(8,128)(2,1)} %multiply_convert_fusion), calls=%async_computation.2 | async-start | bytes 16777216 | tf_op jit(solution)/shard_map/all_to_all | solution.py:143
  263.5 9.9 %reshape.258 = bf16[1280,2048]{1,0:T(8,128)(2,1)} reshape(bf16[128,10,2048]{2,1,0:T(8,128)(2,1)} %all-to-all-done) | data formatting | bytes 10485760 | tf_op jit(solution)/shard_map/reshape | solution.py:112
  273.4 9.7 %fusion.36 = f32[1280,768]{1,0:T(8,128)} fusion(bf16[1280,2048]{1,0:T(8,128)(2,1)} %reshape.258, bf16[1,2048,768]{2,1,0:T(8,128)(2,1)} %param.15), kind=kOutput, calls=%fused_computation.55 | convolution fusion | flops 4026531840 | bytes 12320768 | tf_op jit(solution)/shard_map/dot_general | solution.py:114
  283.2 6.2 fusion.40
  289.3 78.4 %all-to-all-done.2 = bf16[128,10,2048]{2,1,0:T(8,128)(2,1)} async-done(((bf16[128,10,2048]{2,1,0:T(8,128)(2,1)}), bf16[128,10,2048]{2,1,0:T(8,128)(2,1)}, u32[]{:S(2)}, u32[]{:S(2)}) %all-to-all-start.2) | async-done | bytes 5242912 | tf_op jit(solution)/shard_map/all_to_all | solution.py:143
  367.7 9.8 %reshape.262 = bf16[1280,2048]{1,0:T(8,128)(2,1)} reshape(bf16[128,10,2048]{2,1,0:T(8,128)(2,1)} %all-to-all-done.2) | data formatting | bytes 10485760 | tf_op jit(solution)/shard_map/reshape | solution.py:144
  377.5 7.3 %fusion.32 = f32[1280,768]{1,0:T(8,128)S(1)} fusion(bf16[1280,2048]{1,0:T(8,128)(2,1)} %reshape.262, bf16[1,768,2048]{2,1,0:T(8,128)(2,1)} %param.16), kind=kOutput, calls=%fused_computation.51 | convolution fusion | flops 4026531840 | bytes 12320768 | tf_op jit(solution)/shard_map/dot_general | solution.py:147
  384.9 1.9 copy-done.29
  386.8 9.1 %fusion.38 = f32[1280,2048]{1,0:T(8,128)} fusion(bf16[1,2048,768]{2,1,0:T(8,128)(2,1)S(1)} %copy-done, f32[1280,768]{1,0:T(8,128)S(1)} %copy-done.28, f32[1280,768]{1,0:T(8,128)S(1)} %fusion.32, f32[1280,768]{1,0:T(8,128)S(1)} %copy-done.30), kind=kOutput, calls=%fused_computation.57 | convolution fusion | flops 4036362240 | bytes 25427968 | tf_op jit(solution)/shard_map/dot_general | solution.py:153
  395.9 10.6 %add_convert_fusion = bf16[1280,2048]{1,0:T(8,128)(2,1)} fusion(f32[1280,2048]{1,0:T(8,128)} %fusion.38, bf16[1,2048,768]{2,1,0:T(8,128)(2,1)S(1)} %copy-done.27, f32[1280,768]{1,0:T(8,128)} %copy-done.29, f32[1280,768]{1,0:T(8,128)S(1)} %copy-done.28), kind=kOutput, calls=%fused_computation.7 | convolution fusion | flops 4037672960 | bytes 26738688 | tf_op jit(solution)/shard_map/dot_general | solution.py:153
  406.5 9.5 %reshape.263 = bf16[128,10,2048]{2,1,0:T(8,128)(2,1)} reshape(bf16[1280,2048]{1,0:T(8,128)(2,1)} %add_convert_fusion) | data formatting | bytes 10485760 | tf_op jit(solution)/shard_map/reshape | solution.py:157
  416.0 8.6 %all-to-all-start.3 = ((bf16[128,10,2048]{2,1,0:T(8,128)(2,1)}), bf16[128,10,2048]{2,1,0:T(8,128)(2,1)}, u32[]{:S(2)}, u32[]{:S(2)}) async-start(bf16[128,10,2048]{2,1,0:T(8,128)(2,1)} %reshape.263), calls=%async_computation.3 | async-start | bytes 16777216 | tf_op jit(solution)/shard_map/all_to_all | solution.py:156
  424.7 10.9 %convolution_convert_fusion = bf16[1280,2048]{1,0:T(8,128)(2,1)} fusion(bf16[1,768,2048]{2,1,0:T(8,128)(2,1)} %param.16, f32[1280,768]{1,0:T(8,128)} %fusion.36, f32[1280,768]{1,0:T(8,128)} %fusion.40), kind=kOutput, calls=%fused_computation.30 | convolution fusion | flops 4035051520 | bytes 16252928 | tf_op jit(solution)/shard_map/dot_general | solution.py:118
  435.6 9.5 %reshape.259 = bf16[128,10,2048]{2,1,0:T(8,128)(2,1)} reshape(bf16[1280,2048]{1,0:T(8,128)(2,1)} %convolution_convert_fusion) | data formatting | bytes 10485760 | tf_op jit(solution)/shard_map/reshape | solution.py:120
  445.2 82.1 %all-to-all-done.3 = bf16[128,10,2048]{2,1,0:T(8,128)(2,1)} async-done(((bf16[128,10,2048]{2,1,0:T(8,128)(2,1)}), bf16[128,10,2048]{2,1,0:T(8,128)(2,1)}, u32[]{:S(2)}, u32[]{:S(2)}) %all-to-all-start.3) | async-done | bytes 5242912 | tf_op jit(solution)/shard_map/all_to_all | solution.py:156
  527.2 12.2 %all-to-all-start.1 = ((bf16[128,10,2048]{2,1,0:T(8,128)(2,1)}), bf16[128,10,2048]{2,1,0:T(8,128)(2,1)}, u32[]{:S(2)}, u32[]{:S(2)}) async-start(bf16[128,10,2048]{2,1,0:T(8,128)(2,1)} %reshape.259), calls=%async_computation.1 | async-start | bytes 16777216 | tf_op jit(solution)/shard_map/all_to_all | solution.py:124
  539.5 10.0 %reshape.264 = bf16[1280,2048]{1,0:T(8,128)(2,1)} reshape(bf16[128,10,2048]{2,1,0:T(8,128)(2,1)} %all-to-all-done.3) | data formatting | bytes 10485760 | tf_op jit(solution)/shard_map/reshape | solution.py:164
  549.5 12.0 %gather_fusion.4 = bf16[1024,2048]{1,0:T(8,128)(2,1)} fusion(bf16[1280,2048]{1,0:T(8,128)(2,1)} %reshape.264, s32[1024]{0:T(1024)S(1)} %broadcast_clamp_fusion), kind=kCustom, calls=%fused_computation.4 | custom fusion | bytes 8392704 | tf_op jit(solution)/shard_map/gather | solution.py:164
  561.5 5.1 convert_reduce_fusion
  567.9 5.2 fusion.5
  573.1 1.4 convolution_bitcast_fusion.1
  574.5 6.8 fusion.2
  581.4 1.4 convolution_bitcast_fusion
  582.8 1.6 fusion.57
  585.1 1.3 slice-done.5
  586.3 1.6 fusion.60
  588.0 1.1 pad_maximum_fusion
  589.1 3.0 convolution_convert_fusion.2
  592.3 3.0 convolution_convert_fusion.1
  596.2 46.3 %all-to-all-done.1 = bf16[128,10,2048]{2,1,0:T(8,128)(2,1)} async-done(((bf16[128,10,2048]{2,1,0:T(8,128)(2,1)}), bf16[128,10,2048]{2,1,0:T(8,128)(2,1)}, u32[]{:S(2)}, u32[]{:S(2)}) %all-to-all-start.1) | async-done | bytes 5242912 | tf_op jit(solution)/shard_map/all_to_all | solution.py:124
  642.5 9.9 %reshape.260 = bf16[1280,2048]{1,0:T(8,128)(2,1)} reshape(bf16[128,10,2048]{2,1,0:T(8,128)(2,1)} %all-to-all-done.1) | data formatting | bytes 10485760 | tf_op jit(solution)/shard_map/reshape | solution.py:125
  652.3 12.2 %gather_fusion.1 = bf16[1024,2048]{1,0:T(8,128)(2,1)} fusion(bf16[1280,2048]{1,0:T(8,128)(2,1)} %reshape.260, s32[1024]{0:T(1024)S(1)} %broadcast_clamp_fusion), kind=kCustom, calls=%fused_computation.1 | custom fusion | bytes 8392704 | tf_op jit(solution)/shard_map/gather | solution.py:125
  664.6 5.2 fusion.18
  670.6 1.8 pad_maximum_fusion.1
  672.4 7.3 %multiply_reduce_fusion = bf16[128,2048]{1,0:T(8,128)(2,1)} fusion(bf16[1024,2048]{1,0:T(8,128)(2,1)} %gather_fusion.1, f32[128,8]{1,0:T(8,128)S(1)} %copy.36), kind=kLoop, calls=%fused_computation.25 | loop fusion | flops 6029312 | bytes 4722688 | tf_op jit(solution)/shard_map/reduce_sum | solution.py:131
  679.7 17.3 %reduce-scatter.2.cloned.1.call-done = f32[128,256]{0,1:T(8,128)} async-done(((f32[1024,256]{0,1:T(8,128)}), f32[128,256]{0,1:T(8,128)}) %reduce-scatter.2.cloned.1.call-update) | async-done | bytes 131088 | tf_op jit(solution)/shard_map/reduce_scatter | solution.py:226
  697.0 0.9 convert.20
  (129 shorter events, 11.5 us)
Async XLA Ops:
  7.2 276.0 %copy-start = (bf16[1,2048,768]{2,1,0:T(8,128)(2,1)S(1)}, bf16[1,2048,768]{2,1,0:T(8,128)(2,1)}, u32[]{:S(2)}) copy-start(bf16[1,2048,768]{2,1,0:T(8,128)(2,1)} %param.14) | copy-start | bytes 9437188
  9.7 92.7 %copy-start.12 = (pred[128,1024]{0,1:T(8,128)(4,1)}, pred[128,1024]{0,1:T(8,128)(4,1)S(1)}, u32[]{:S(2)}) copy-start(pred[128,1024]{0,1:T(8,128)(4,1)S(1)} %iota_compare_fusion.2) | copy-start | bytes 393220
  45.8 18.6 %copy-start.8 = (bf16[128,1024]{0,1:T(8,128)(2,1)}, bf16[128,1024]{0,1:T(8,128)(2,1)S(1)}, u32[]{:S(2)}) copy-start(bf16[128,1024]{0,1:T(8,128)(2,1)S(1)} %copy.38) | copy-start | bytes 786436
  65.3 35.0 %copy-start.4 = (f32[1024,128,16]{1,0,2:T(8,128)S(1)}, f32[1024,128,16]{1,0,2:T(8,128)}, u32[]{:S(2)}) copy-start(f32[1024,128,16]{1,0,2:T(8,128)} %get-tuple-element.43) | copy-start | bytes 25165828
  95.7 6.6 copy-start.15
  95.7 6.6 slice-start
  100.3 2.2 slice-start.1
  100.3 2.2 copy-start.22
  102.6 2.0 copy-start.23
  104.6 6.3 copy-start.19
  108.2 21.3 %copy-start.24 = (f32[128]{0:T(128)}, f32[128]{0:T(128)S(1)}, u32[]{:S(2)}) copy-start(f32[128]{0:T(128)S(1)} %get-tuple-element.40) | copy-start | bytes 1540
  108.5 0.8 copy-start.10
  139.1 9.4 %copy-start.17 = (f32[1,128,8]{1,2,0:T(8,128)S(1)}, f32[1,128,8]{1,2,0:T(8,128)}, u32[]{:S(2)}) copy-start(f32[1,128,8]{1,2,0:T(8,128)} %param.13) | copy-start | bytes 12292
  139.1 112.0 %all-to-all-start = ((bf16[128,10,2048]{2,1,0:T(8,128)(2,1)}), bf16[128,10,2048]{2,1,0:T(8,128)(2,1)}, u32[]{:S(2)}, u32[]{:S(2)}) async-start(bf16[128,10,2048]{2,1,0:T(8,128)(2,1)} %reshape.257), calls=%async_computation | async-start | bytes 16777216 | tf_op jit(solution)/shard_map/all_to_all | solution.py:109
  148.6 0.5 copy-start.20
  251.1 116.6 %all-to-all-start.2 = ((bf16[128,10,2048]{2,1,0:T(8,128)(2,1)}), bf16[128,10,2048]{2,1,0:T(8,128)(2,1)}, u32[]{:S(2)}, u32[]{:S(2)}) async-start(bf16[128,10,2048]{2,1,0:T(8,128)(2,1)} %multiply_convert_fusion), calls=%async_computation.2 | async-start | bytes 16777216 | tf_op jit(solution)/shard_map/all_to_all | solution.py:143
  273.4 9.7 %copy-start.6 = (bf16[1280,2048]{1,0:T(8,128)(2,1)S(1)}, bf16[1280,2048]{1,0:T(8,128)(2,1)}, u32[]{:S(2)}) copy-start(bf16[1280,2048]{1,0:T(8,128)(2,1)} %reshape.258) | copy-start | bytes 15728644
  377.5 9.3 %copy-start.28 = (f32[1280,768]{1,0:T(8,128)S(1)}, f32[1280,768]{1,0:T(8,128)}, u32[]{:S(2)}) copy-start(f32[1280,768]{1,0:T(8,128)} %fusion.40) | copy-start | bytes 11796484
  377.5 9.3 %copy-start.30 = (f32[1280,768]{1,0:T(8,128)S(1)}, f32[1280,768]{1,0:T(8,128)}, u32[]{:S(2)}) copy-start(f32[1280,768]{1,0:T(8,128)} %fusion.36) | copy-start | bytes 11796484
  384.9 1.9 copy-start.29
  386.8 9.1 %copy-start.27 = (bf16[1,2048,768]{2,1,0:T(8,128)(2,1)S(1)}, bf16[1,2048,768]{2,1,0:T(8,128)(2,1)}, u32[]{:S(2)}) copy-start(bf16[1,2048,768]{2,1,0:T(8,128)(2,1)} %param.15) | copy-start | bytes 9437188
  416.0 8.6 %copy-start.7 = (bf16[128,32,64]{0,2,1:T(8,128)(2,1)S(1)}, bf16[128,32,64]{0,2,1:T(8,128)(2,1)}, u32[]{:S(2)}) copy-start(bf16[128,32,64]{0,2,1:T(8,128)(2,1)} %get-tuple-element.20) | copy-start | bytes 1572868
  416.0 111.2 %all-to-all-start.3 = ((bf16[128,10,2048]{2,1,0:T(8,128)(2,1)}), bf16[128,10,2048]{2,1,0:T(8,128)(2,1)}, u32[]{:S(2)}, u32[]{:S(2)}) async-start(bf16[128,10,2048]{2,1,0:T(8,128)(2,1)} %reshape.263), calls=%async_computation.3 | async-start | bytes 16777216 | tf_op jit(solution)/shard_map/all_to_all | solution.py:156
  527.2 115.2 %all-to-all-start.1 = ((bf16[128,10,2048]{2,1,0:T(8,128)(2,1)}), bf16[128,10,2048]{2,1,0:T(8,128)(2,1)}, u32[]{:S(2)}, u32[]{:S(2)}) async-start(bf16[128,10,2048]{2,1,0:T(8,128)(2,1)} %reshape.259), calls=%async_computation.1 | async-start | bytes 16777216 | tf_op jit(solution)/shard_map/all_to_all | solution.py:124
  539.5 157.5 %reduce-scatter.2.cloned.1.call-start = ((), (), s32[]{:S(2)}) async-start(), calls=%async_computation.5 | async-start | bytes 1179648 | tf_op jit(solution)/shard_map/reduce_scatter | solution.py:226
  561.5 5.1 copy-start.5
  561.5 5.3 copy-start.25
  561.5 5.3 copy-start.26
  561.5 6.3 copy-start.13
  567.9 5.2 copy-start.9
  573.1 8.2 %copy-start.2 = (bf16[16,128,1024]{1,2,0:T(8,128)(2,1)}, bf16[16,128,1024]{1,2,0:T(8,128)(2,1)S(1)}, u32[]{:S(2)}) copy-start(bf16[16,128,1024]{1,2,0:T(8,128)(2,1)S(1)} %fusion.5) | copy-start | bytes 12582916
  573.1 1.4 copy-start.16
  573.1 9.6 %slice-start.2 = ((s8[8388608]{0:T(1024)(128)(4,1)}), s8[4194304]{0:T(1024)(128)(4,1)S(1)}, s32[]{:S(2)}) async-start(s8[8388608]{0:T(1024)(128)(4,1)} %bitcast.208), calls=%async_computation.8 | async-start | bytes 8388608
  574.5 6.8 copy-start.14
  574.5 8.2 %slice-start.3 = ((s8[8388608]{0:T(1024)(128)(4,1)}), s8[4194304]{0:T(1024)(128)(4,1)S(1)}, s32[]{:S(2)}) async-start(s8[8388608]{0:T(1024)(128)(4,1)} %bitcast.208), calls=%async_computation.9 | async-start | bytes 8388608
  581.4 3.1 copy-start.3
  581.4 3.7 slice-start.4
  582.8 3.6 slice-start.5
  586.3 2.7 copy-start.11
  664.6 5.3 copy-start.18
  664.6 5.3 copy-start.21
  664.6 34.7 %copy-start.1 = (bf16[1,2048,768]{2,1,0:T(8,128)(2,1)S(1)}, bf16[1,2048,768]{2,1,0:T(8,128)(2,1)}, u32[]{:S(2)}) copy-start(bf16[1,2048,768]{2,1,0:T(8,128)(2,1)} %param.14) | copy-start | bytes 9437188
Sparse Core Ops, SparseCore 0:
  589.2 107.7 reduce-scatter.1
where the time goes:
time: 714 us; the launch traced here: 706 us
  waiting for transfers between devices  285 us (40%)
  local copies, waits for them, and re-layouts  160 us (22%)
  matrix products  103 us (14%)
  blocking collectives  62.7 us (9%)
  starting transfers between devices  42.7 us (6%)
  other arithmetic  37.7 us (5%)
  between operations  15 us (2%)
    all_to_all x1, waiting for transfers between devices, shards(): lax.all_to_all(row_grad.astype(jnp.bfloat16).reshape(arrived_grad.shape),...  82.1 us
    all_to_all x1, waiting for transfers between devices, shards(): lax.all_to_all(grad_sent, ('dp', 'ctx'), split_axis=0, concat_axis=0, til...  78.4 us
    all_to_all x1, waiting for transfers between devices, shards(): lax.all_to_all(outgoing, ('dp', 'ctx'), split_axis=0, concat_axis=0, tile...  61.2 us
    all_to_all x1, waiting for transfers between devices, shards(): lax.all_to_all(produced, ('dp', 'ctx'), split_axis=0, concat_axis=0, tile...  46.3 us
    all_gather x1, blocking collectives, shards(): block_keys = lax.all_gather(keys, 'ctx', axis=1, tiled=True)[0]  32.3 us
    all_gather x1, blocking collectives, shards(): block_values = lax.all_gather(values, 'ctx', axis=1, tiled=True)[0]  30.4 us
    reduce_scatter x1, waiting for transfers between devices, shards(): lax.psum_scatter(jnp.concatenate(key_parts + value_parts, axis=1), 'ctx',...  17.3 us
    dot_general x2, matrix products, shards(): jnp.einsum('thd,sd->hts', query_sets[fold_head_set], block_keys[:, fold_h...  16.2 us
  transfers between devices with their start and end apart: 5, of which 5 were waited for; matrix products, arithmetic and copies ran while one was open for 25% of the time, Pallas kernels for 0%

commit v1 on v0

--- a/solution.py
+++ b/solution.py
@@ -1,6 +1,10 @@
+import functools
+
 import jax
 import jax.numpy as jnp
 from jax import lax
+from jax.experimental import pallas as pl
+from jax.experimental.pallas import tpu as pltpu
 from jax.sharding import PartitionSpec as P
 
 KVH = 2
@@ -11,6 +15,83 @@
 
 EPSILON = 1e-06
 NEGATIVE = -1e30
+
+
+MESH = pl.DeviceIdType.MESH
+CHUNK_ROWS = 16
+
+
+def offset_target(step, x, y, z, core, sign):
+    inner = step % 64
+    a, b, c = inner // 16, (inner // 4) % 4, inner % 4
+    dx = c
+    dy = (c + b) % 4
+    dz = (c + a + 2 * b) % 4
+    tx = (x + sign * dx + 4) % 4
+    ty = (y + sign * dy + 4) % 4
+    tz = (z + sign * dz + 4) % 4
+    tcore = (core + step // 64) % 2
+    return tx * 4 + (tz % 2) * 2 + tcore, ty * 2 + tz // 2
+
+
+def exchange_kernel(count, src, dst, send_sem, recv_sem, own_sem):
+    dp, ctx = lax.axis_index("dp"), lax.axis_index("ctx")
+    x, core = dp // 4, dp % 2
+    y, z = ctx // 2, (dp // 2) % 2 + 2 * (ctx % 2)
+    sign = 1 - 2 * core
+    me = dp * 8 + ctx
+    barrier = pltpu.get_barrier_semaphore()
+
+    def greet(step, carry):
+        tdp, tctx = offset_target(step, x, y, z, core, sign)
+        pl.semaphore_signal(barrier, inc=1, device_id=(tdp, tctx), device_id_type=MESH)
+        return carry
+
+    lax.fori_loop(1, count, greet, 0)
+    pl.semaphore_wait(barrier, count - 1)
+    own = pltpu.make_async_copy(src.at[me], dst.at[me], own_sem)
+    own.start()
+
+    def send(step, carry):
+        tdp, tctx = offset_target(step, x, y, z, core, sign)
+        pltpu.make_async_remote_copy(
+            src_ref=src.at[tdp * 8 + tctx],
+            dst_ref=dst.at[me],
+            send_sem=send_sem,
+            recv_sem=recv_sem,
+            device_id=(tdp, tctx),
+            device_id_type=MESH,
+        ).start()
+        return carry
+
+    lax.fori_loop(1, count, send, 0)
+    tdp, tctx = offset_target(1, x, y, z, core, sign)
+    everything = pltpu.make_async_remote_copy(
+        src_ref=src.at[pl.ds(0, count - 1)],
+        dst_ref=dst.at[pl.ds(0, count - 1)],
+        send_sem=send_sem,
+        recv_sem=recv_sem,
+        device_id=(tdp, tctx),
+        device_id_type=MESH,
+    )
+    everything.wait()
+    own.wait()
+
+
+def exchange(rows, number):
+    count = rows.shape[0]
+    size = rows.shape[1] * rows.shape[2]
+    flat = rows.reshape(count, CHUNK_ROWS, size // CHUNK_ROWS)
+    out = pl.pallas_call(
+        functools.partial(exchange_kernel, count),
+        out_shape=jax.ShapeDtypeStruct(flat.shape, flat.dtype),
+        in_specs=[pl.BlockSpec(memory_space=pl.ANY)],
+        out_specs=pl.BlockSpec(memory_space=pl.ANY),
+        scratch_shapes=[pltpu.SemaphoreType.DMA] * 3,
+        compiler_params=pltpu.CompilerParams(collective_id=number, has_side_effects=True),
+        name="exchange_%d" % number,
+    )(flat)
+    return out.reshape(rows.shape)
 
 
 def shards(
@@ -106,7 +187,7 @@
     w_gate = gate_weight[0]
     w_up = up_weight[0]
     w_down = down_weight[0]
-    arrived_rows = lax.all_to_all(outgoing, ("dp", "ctx"), split_axis=0, concat_axis=0, tiled=True)
+    arrived_rows = exchange(outgoing, 0)
     sources = arrived_rows.shape[0]
     slots = arrived_rows.shape[1]
     flat_rows = arrived_rows.reshape(sources * slots, model_width)
@@ -121,7 +202,7 @@
         expert_gate_act.reshape(sources, slots, -1),
         expert_up_act.reshape(sources, slots, -1),
     )
-    returned = lax.all_to_all(produced, ("dp", "ctx"), split_axis=0, concat_axis=0, tiled=True)
+    returned = exchange(produced, 1)
     pick_out = returned.reshape(experts * capacity, model_width)[placed].reshape(
         rows_here, TOPK, model_width
     )
@@ -140,7 +221,7 @@
         .astype(jnp.bfloat16)
         .reshape(experts, capacity, model_width)
     )
-    arrived_grad = lax.all_to_all(grad_sent, ("dp", "ctx"), split_axis=0, concat_axis=0, tiled=True)
+    arrived_grad = exchange(grad_sent, 2)
     flat_grad = arrived_grad.reshape(-1, model_width)
     gate_flat = gate_act.reshape(flat_grad.shape[0], -1)
     up_flat = up_act.reshape(flat_grad.shape[0], -1)
@@ -153,13 +234,7 @@
     row_grad = jnp.dot(gate_grad, w_gate.T, preferred_element_type=jnp.float32) + jnp.dot(
         up_grad, w_up.T, preferred_element_type=jnp.float32
     )
-    returned_grad = lax.all_to_all(
-        row_grad.astype(jnp.bfloat16).reshape(arrived_grad.shape),
-        ("dp", "ctx"),
-        split_axis=0,
-        concat_axis=0,
-        tiled=True,
-    )
+    returned_grad = exchange(row_grad.astype(jnp.bfloat16).reshape(arrived_grad.shape), 3)
     normed_grad = jnp.sum(
         returned_grad.reshape(experts * capacity, model_width)[placed]
         .reshape(rows_here, TOPK, model_width)

time: 714 us -> 661 us (0.926)
  waiting for transfers between devices: 285 us -> 0.02 us
  Pallas kernels: 0 us -> 284 us
  starting transfers between devices: 42.7 us -> 0.04 us
  matrix products: 103 us -> 90.6 us
  other arithmetic: 37.7 us -> 30.5 us
    pallas_call x0 -> x4, Pallas kernels: none -> 284 us  [exchange(): pl.pallas_call(functools.partial(exchange_kernel, count), out_shape=jax.S...]
    all_to_all x4 -> x0, waiting for transfers between devices: 268 us -> none  [the longest x1 82.1 us: shards(): lax.all_to_all(row_grad.astype(jnp.bfloat16).reshape(arrived_grad.shape),...]
    another operation x3 -> x10, local copies, waits for them, and re-layouts: 0.11 us -> 69 us  [the longest x3 29.7 us: exchange(): flat = rows.reshape(count, CHUNK_ROWS, size // CHUNK_ROWS)]
    reshape x7 -> x0, local copies, waits for them, and re-layouts: 68.2 us -> none  [the longest x1 10 us: shards(): returned_grad.reshape(experts * capacity, model_width)[placed]]
    all_to_all x4 -> x0, starting transfers between devices: 42.7 us -> none  [the longest x1 12.4 us: shards(): lax.all_to_all(grad_sent, ('dp', 'ctx'), split_axis=0, concat_axis=0, til...]
    reduce_scatter x1, waiting for transfers between devices: 17.3 us -> 0.01 us  [shards(): lax.psum_scatter(jnp.concatenate(key_parts + value_parts, axis=1), 'ctx',...]
    dot_general x2, matrix products: 16.2 us -> 5.45 us  [shards(): jnp.einsum('thd,sd->hts', query_sets[fold_head_set], block_keys[:, fold_h...]
  transfers between devices with their start and end apart: 5 -> 1, of which waited for: 5 -> 0; matrix products, arithmetic and copies ran while one was open for 25% -> 10% of each run, Pallas kernels for 0% -> 11%
where the time goes in v1:
time: 661 us; the launch traced here: 648 us
  Pallas kernels  284 us (43%)
  local copies, waits for them, and re-layouts  164 us (25%)
  matrix products  90.6 us (14%)
  blocking collectives  64.1 us (10%)
  other arithmetic  30.5 us (5%)
  between operations  15.2 us (2%)
    pallas_call x4, Pallas kernels, exchange(): pl.pallas_call(functools.partial(exchange_kernel, count), out_shape=jax.S...  284 us
    all_gather x1, blocking collectives, shards(): block_values = lax.all_gather(values, 'ctx', axis=1, tiled=True)[0]  32.3 us
    all_gather x1, blocking collectives, shards(): block_keys = lax.all_gather(keys, 'ctx', axis=1, tiled=True)[0]  31.8 us
    another operation x3, local copies, waits for them, and re-layouts, exchange(): flat = rows.reshape(count, CHUNK_ROWS, size // CHUNK_ROWS)  29.7 us
  transfers between devices with their start and end apart: 1, of which 0 were waited for; matrix products, arithmetic and copies ran while one was open for 10% of the time, Pallas kernels for 11%

profile of v1, /device:TPU:0, one launch (start us, length us, event | category | flops | bytes accessed | tf_op | source)
XLA Modules:
  0.0 648.5 jit_solution(16437783635173416599)
XLA Ops:
  7.2 0.8 broadcast_multiply_fusion
  8.1 0.8 copy.45
  9.1 0.9 copy.37
  10.0 0.9 copy.39
  11.0 32.3 %all_gather.9 = bf16[1,1024,128]{1,2,0:T(8,128)(2,1)} all-gather(bf16[1,128,128]{1,2,0:T(8,128)(2,1)S(1)} %copy.39), channel_id=1, replica_groups=mesh['dp'=16,'ctx'=8] {'ctx'}, dimensions={1}, use_global_device_ids=true | all-gather | bytes 294912 | tf_op jit(solution)/shard_map/all_gather | solution.py:115
  43.2 31.8 %all_gather.8 = bf16[1,1024,128]{1,2,0:T(8,128)(2,1)} all-gather(bf16[1,128,128]{1,2,0:T(8,128)(2,1)S(1)} %copy.37), channel_id=1, replica_groups=mesh['dp'=16,'ctx'=8] {'ctx'}, dimensions={1}, use_global_device_ids=true | all-gather | bytes 294912 | tf_op jit(solution)/shard_map/all_gather | solution.py:114
  75.1 1.9 fusion.102
  76.9 1.1 copy.38
  78.1 1.9 copy.41
  80.0 2.3 fusion.10
  82.3 3.2 fusion.14
  85.5 1.9 fusion.54
  87.5 2.2 fusion.16
  89.7 1.9 fusion.51
  91.7 1.0 multiply_reduce_fusion.1
  92.7 2.0 copy.43
  94.8 1.9 fusion.101
  98.4 1.1 broadcast_add_fusion
  100.0 4.3 scatter_custom_fusion
  104.4 7.3 %gather_fusion.2 = f32[1280]{0:T(1024)S(1)} fusion(f32[1025]{0:T(1024)S(1)} %pad_maximum_fusion.3, s32[2048]{0:T(1024)S(1)} %get-tuple-element.44), kind=kCustom, calls=%fused_computation.2 | custom fusion | bytes 15360 | tf_op jit(solution)/shard_map/gather | solution.py:220
  111.7 1.9 concatenate.42
  113.6 11.9 %gather_fusion.3 = bf16[1280,2048]{1,0:T(8,128)(2,1)} fusion(bf16[129,2048]{1,0:T(8,128)(2,1)} %concatenate.42, s32[2048]{0:T(1024)S(1)} %get-tuple-element.45), kind=kCustom, calls=%fused_computation.3 | custom fusion | bytes 10490880 | tf_op jit(solution)/shard_map/gather | solution.py:220
  125.6 5.7 multiply_convert_fusion
  131.3 9.8 %convert_element_type.142.src = bf16[128,16,1280]{2,1,0:T(8,128)(2,1)} reshape(bf16[1280,2048]{1,0:T(8,128)(2,1)} %multiply_convert_fusion) | data formatting | bytes 10485760 | tf_op jit(solution)/shard_map/convert_element_type | solution.py:221
  141.1 70.4 %exchange_2.1 = bf16[128,16,1280]{2,1,0:T(8,128)(2,1)} custom-call(bf16[128,16,1280]{2,1,0:T(8,128)(2,1)} %convert_element_type.142.src), custom_call_target="tpu_custom_call" | custom-call | tf_op jit(solution)/shard_map/exchange_2/pallas_call | solution.py:85
  211.5 9.8 %reshape_reshape.26 = bf16[1280,2048]{1,0:T(8,128)(2,1)} reshape(bf16[128,16,1280]{2,1,0:T(8,128)(2,1)} %exchange_2.1) | data formatting | bytes 10485760 | tf_op jit(solution)/shard_map/reshape;reshape | solution.py:225
  221.9 1.2 fusion.63
  223.1 0.9 concatenate.39
  224.0 11.9 %gather_fusion = bf16[1280,2048]{1,0:T(8,128)(2,1)} fusion(bf16[129,2048]{1,0:T(8,128)(2,1)} %concatenate.39, s32[2048]{0:T(1024)S(1)} %get-tuple-element.45), kind=kCustom, calls=%fused_computation | custom fusion | bytes 10490880 | tf_op jit(solution)/shard_map/gather | solution.py:186
  235.9 9.9 %reshape_reshape.22.src = bf16[128,16,1280]{2,1,0:T(8,128)(2,1)} reshape(bf16[1280,2048]{1,0:T(8,128)(2,1)} %gather_fusion) | data formatting | bytes 10485760 | tf_op jit(solution)/shard_map/reshape;reshape | solution.py:84
  245.8 70.2 %exchange_0.1 = bf16[128,16,1280]{2,1,0:T(8,128)(2,1)} custom-call(bf16[128,16,1280]{2,1,0:T(8,128)(2,1)} %reshape_reshape.22.src), custom_call_target="tpu_custom_call" | custom-call | tf_op jit(solution)/shard_map/exchange_0/pallas_call | solution.py:85
  316.0 9.8 %reshape_reshape.23 = bf16[1280,2048]{1,0:T(8,128)(2,1)} reshape(bf16[128,16,1280]{2,1,0:T(8,128)(2,1)} %exchange_0.1) | data formatting | bytes 10485760 | tf_op jit(solution)/shard_map/reshape;reshape | solution.py:193
  325.9 7.0 %fusion.40 = f32[1280,768]{1,0:T(8,128)S(1)} fusion(bf16[1280,2048]{1,0:T(8,128)(2,1)} %reshape_reshape.23, bf16[1,2048,768]{2,1,0:T(8,128)(2,1)S(1)} %copy-done), kind=kOutput, calls=%fused_computation.59 | convolution fusion | flops 4026531840 | bytes 12320768 | tf_op jit(solution)/shard_map/dot_general | solution.py:194
  332.9 6.2 fusion.36
  339.1 4.4 fusion.32
  343.5 1.9 copy-done.28
  345.4 11.2 %fusion.38 = f32[1280,2048]{1,0:T(8,128)} fusion(bf16[1,2048,768]{2,1,0:T(8,128)(2,1)S(1)} %copy-done, f32[1280,768]{1,0:T(8,128)S(1)} %fusion.40, f32[1280,768]{1,0:T(8,128)S(1)} %fusion.32, f32[1280,768]{1,0:T(8,128)} %fusion.36), kind=kOutput, calls=%fused_computation.57 | convolution fusion | flops 4036362240 | bytes 25427968 | tf_op jit(solution)/shard_map/dot_general | solution.py:234
  356.6 11.1 %add_convert_fusion = bf16[1280,2048]{1,0:T(8,128)(2,1)} fusion(f32[1280,2048]{1,0:T(8,128)} %fusion.38, bf16[1,2048,768]{2,1,0:T(8,128)(2,1)S(1)} %copy-done.25, f32[1280,768]{1,0:T(8,128)} %copy-done.28, f32[1280,768]{1,0:T(8,128)} %copy-done.27), kind=kOutput, calls=%fused_computation.6 | convolution fusion | flops 4037672960 | bytes 26738688 | tf_op jit(solution)/shard_map/dot_general | solution.py:234
  367.7 10.0 %reshape_reshape.27.src = bf16[128,16,1280]{2,1,0:T(8,128)(2,1)} reshape(bf16[1280,2048]{1,0:T(8,128)(2,1)} %add_convert_fusion) | data formatting | bytes 10485760 | tf_op jit(solution)/shard_map/reshape;reshape | solution.py:84
  377.7 71.5 %exchange_3.1 = bf16[128,16,1280]{2,1,0:T(8,128)(2,1)} custom-call(bf16[128,16,1280]{2,1,0:T(8,128)(2,1)} %reshape_reshape.27.src), custom_call_target="tpu_custom_call" | custom-call | tf_op jit(solution)/shard_map/exchange_3/pallas_call | solution.py:85
  449.2 9.8 %reshape_reshape.28 = bf16[1280,2048]{1,0:T(8,128)(2,1)} reshape(bf16[128,16,1280]{2,1,0:T(8,128)(2,1)} %exchange_3.1) | data formatting | bytes 10485760 | tf_op jit(solution)/shard_map/reshape;reshape | solution.py:239
  459.0 12.0 %gather_fusion.4 = bf16[1024,2048]{1,0:T(8,128)(2,1)} fusion(bf16[1280,2048]{1,0:T(8,128)(2,1)} %reshape_reshape.28, s32[1024]{0:T(1024)S(1)} %broadcast_clamp_fusion), kind=kCustom, calls=%fused_computation.4 | custom fusion | bytes 8392704 | tf_op jit(solution)/shard_map/gather | solution.py:239
  471.0 5.1 convert_reduce_fusion
  477.2 5.2 fusion.60
  482.4 5.5 fusion.2
  488.0 1.4 convolution_bitcast_fusion
  489.5 1.6 fusion.57
  491.2 3.1 fusion.5
  494.2 2.1 copy-done.3
  496.3 1.4 convolution_bitcast_fusion.1
  497.7 1.1 pad_maximum_fusion
  498.8 10.8 %convolution_convert_fusion = bf16[1280,2048]{1,0:T(8,128)(2,1)} fusion(bf16[1,768,2048]{2,1,0:T(8,128)(2,1)} %param.16, f32[1280,768]{1,0:T(8,128)} %fusion.36, f32[1280,768]{1,0:T(8,128)} %copy-done.27), kind=kOutput, calls=%fused_computation.30 | convolution fusion | flops 4035051520 | bytes 16252928 | tf_op jit(solution)/shard_map/dot_general | solution.py:199
  509.7 9.8 %reshape_reshape.24.src = bf16[128,16,1280]{2,1,0:T(8,128)(2,1)} reshape(bf16[1280,2048]{1,0:T(8,128)(2,1)} %convolution_convert_fusion) | data formatting | bytes 10485760 | tf_op jit(solution)/shard_map/reshape;reshape | solution.py:84
  519.5 71.9 %exchange_1.1 = bf16[128,16,1280]{2,1,0:T(8,128)(2,1)} custom-call(bf16[128,16,1280]{2,1,0:T(8,128)(2,1)} %reshape_reshape.24.src), custom_call_target="tpu_custom_call" | custom-call | tf_op jit(solution)/shard_map/exchange_1/pallas_call | solution.py:85
  591.4 9.8 %reshape_reshape.25 = bf16[1280,2048]{1,0:T(8,128)(2,1)} reshape(bf16[128,16,1280]{2,1,0:T(8,128)(2,1)} %exchange_1.1) | data formatting | bytes 10485760 | tf_op jit(solution)/shard_map/reshape;reshape | solution.py:206
  601.1 12.3 %gather_fusion.1 = bf16[1024,2048]{1,0:T(8,128)(2,1)} fusion(bf16[1280,2048]{1,0:T(8,128)(2,1)} %reshape_reshape.25, s32[1024]{0:T(1024)S(1)} %broadcast_clamp_fusion), kind=kCustom, calls=%fused_computation.1 | custom fusion | bytes 8392704 | tf_op jit(solution)/shard_map/gather | solution.py:206
  613.4 4.9 fusion.18
  618.6 3.8 convolution_convert_fusion.1
  622.4 1.9 copy.58
  624.3 3.7 convolution_convert_fusion.2
  628.0 1.1 copy.57
  629.7 1.8 pad_maximum_fusion.1
  631.5 7.3 %multiply_reduce_fusion = bf16[128,2048]{1,0:T(8,128)(2,1)} fusion(bf16[1024,2048]{1,0:T(8,128)(2,1)} %gather_fusion.1, f32[128,8]{1,0:T(8,128)S(1)} %copy.36), kind=kLoop, calls=%fused_computation.25 | loop fusion | flops 6029312 | bytes 4722688 | tf_op jit(solution)/shard_map/reduce_sum | solution.py:212
  638.8 0.9 convert.19
  (115 shorter events, 6.8 us)
Async XLA Ops:
  7.2 318.7 %copy-start = (bf16[1,2048,768]{2,1,0:T(8,128)(2,1)S(1)}, bf16[1,2048,768]{2,1,0:T(8,128)(2,1)}, u32[]{:S(2)}) copy-start(bf16[1,2048,768]{2,1,0:T(8,128)(2,1)} %param.14) | copy-start | bytes 9437188
  7.2 631.7 %reduce-scatter.2.cloned.1.call-start = ((), (), s32[]{:S(2)}) async-start(), calls=%async_computation.1 | async-start | bytes 1179648 | tf_op jit(solution)/shard_map/reduce_scatter | solution.py:301
  78.1 7.4 %copy-start.8 = (bf16[128,1024]{0,1:T(8,128)(2,1)}, bf16[128,1024]{0,1:T(8,128)(2,1)S(1)}, u32[]{:S(2)}) copy-start(bf16[128,1024]{0,1:T(8,128)(2,1)S(1)} %copy.38) | copy-start | bytes 786436
  80.0 2.3 copy-start.11
  80.0 2.3 copy-start.13
  82.2 3.3 copy-start.4
  82.3 3.3 copy-start.18
  85.5 4.2 copy-start.5
  89.7 6.9 %copy-start.20 = (f32[1,128,8]{1,2,0:T(8,128)S(1)}, f32[1,128,8]{1,2,0:T(8,128)}, u32[]{:S(2)}) copy-start(f32[1,128,8]{1,2,0:T(8,128)} %param.13) | copy-start | bytes 12292
  96.8 0.8 copy-start.22
  97.6 0.8 copy-start.10
  325.9 7.0 %copy-start.7 = (bf16[1280,2048]{1,0:T(8,128)(2,1)S(1)}, bf16[1280,2048]{1,0:T(8,128)(2,1)}, u32[]{:S(2)}) copy-start(bf16[1280,2048]{1,0:T(8,128)(2,1)} %reshape_reshape.23) | copy-start | bytes 15728644
  325.9 7.0 %copy-start.25 = (bf16[1,2048,768]{2,1,0:T(8,128)(2,1)S(1)}, bf16[1,2048,768]{2,1,0:T(8,128)(2,1)}, u32[]{:S(2)}) copy-start(bf16[1,2048,768]{2,1,0:T(8,128)(2,1)} %param.15) | copy-start | bytes 9437188
  325.9 13.2 %slice-start.2 = ((s8[5242880]{0:T(1024)(128)(4,1)}), s8[4194304]{0:T(1024)(128)(4,1)S(1)}, s32[]{:S(2)}) async-start(s8[5242880]{0:T(1024)(128)(4,1)} %bitcast.209), calls=%async_computation.4 | async-start | bytes 8388608
  332.9 10.6 %copy-start.27 = (f32[1280,768]{1,0:T(8,128)}, f32[1280,768]{1,0:T(8,128)S(1)}, u32[]{:S(2)}) copy-start(f32[1280,768]{1,0:T(8,128)S(1)} %fusion.40) | copy-start | bytes 11796484
  332.9 6.2 slice-start.3
  332.9 6.2 copy-start.26
  343.5 1.9 copy-start.28
  471.0 5.1 copy-start.6
  471.0 6.1 copy-start.16
  471.0 6.2 copy-start.24
  477.2 5.2 copy-start.19
  477.2 12.3 %slice-start = ((s8[8388608]{0:T(1024)(128)(4,1)}), s8[4194304]{0:T(1024)(128)(4,1)S(1)}, s32[]{:S(2)}) async-start(s8[8388608]{0:T(1024)(128)(4,1)} %bitcast.207), calls=%async_computation.2 | async-start | bytes 8388608
  482.4 5.6 copy-start.14
  482.4 7.1 %slice-start.1 = ((s8[8388608]{0:T(1024)(128)(4,1)}), s8[4194304]{0:T(1024)(128)(4,1)S(1)}, s32[]{:S(2)}) async-start(s8[8388608]{0:T(1024)(128)(4,1)} %bitcast.207), calls=%async_computation.3 | async-start | bytes 8388608
  488.0 3.2 copy-start.2
  488.0 1.4 copy-start.15
  491.2 5.1 copy-start.9
  494.2 2.1 copy-start.3
  601.1 12.3 %copy-start.17 = (bf16[1,128,2048]{2,1,0:T(8,128)(2,1)S(1)}, bf16[1,128,2048]{2,1,0:T(8,128)(2,1)}, u32[]{:S(2)}) copy-start(bf16[1,128,2048]{2,1,0:T(8,128)(2,1)} %param.17) | copy-start | bytes 1572868
  613.4 5.0 copy-start.21
  613.4 5.0 copy-start.23
  613.4 5.2 copy-start.12
  622.4 18.8 %copy-start.1 = (bf16[1,2048,768]{2,1,0:T(8,128)(2,1)S(1)}, bf16[1,2048,768]{2,1,0:T(8,128)(2,1)}, u32[]{:S(2)}) copy-start(bf16[1,2048,768]{2,1,0:T(8,128)(2,1)} %param.14) | copy-start | bytes 9437188
Sparse Core Ops, SparseCore 0:
  498.9 123.9 reduce-scatter.1

commit v2 on v0

v2 whole, which is shorter than its diff:
```python
import functools

import jax
import jax.numpy as jnp
from jax import lax
from jax.experimental import pallas as pl
from jax.experimental.pallas import tpu as pltpu
from jax.sharding import PartitionSpec as P

HD = 64
EPSILON = 1e-06
NEGATIVE = -1e30
MESH = pl.DeviceIdType.MESH
F32 = jnp.float32
BF16 = jnp.bfloat16

ROWS = 16
MAIN = 1024
SPILL = 256
CHUNK = MAIN + SPILL
BLOCK = 16
PAIR = 128


def dot(a, b):
    return lax.dot_general(a, b, (((1,), (0,)), ((), ())), preferred_element_type=F32)


def dot_nt(a, b):
    return lax.dot_general(a, b, (((1,), (1,)), ((), ())), preferred_element_type=F32)


def iota(shape, dim):
    return lax.broadcasted_iota(jnp.int32, shape, dim)


def torus_partner(step, x, y, z, core, sign):
    inner = step % 64
    a, b, c = inner // 16, (inner // 4) % 4, inner % 4
    dx = c
    dy = (c + b) % 4
    dz = (c + a + 2 * b) % 4
    tx = (x + sign * dx + 4) % 4
    ty = (y + sign * dy + 4) % 4
    tz = (z + sign * dz + 4) % 4
    tcore = (core + step // 64) % 2
    return tx * 4 + (tz % 2) * 2 + tcore, ty * 2 + tz // 2


def partners(n_dp, n_ctx):
    dp, ctx = lax.axis_index("dp"), lax.axis_index("ctx")
    count = n_dp * n_ctx
    if (n_dp, n_ctx) == (16, 8):
        x, core = dp // 4, dp % 2
        y, z = ctx // 2, (dp // 2) % 2 + 2 * (ctx % 2)
        sign = 1 - 2 * core

        def target(step):
            return torus_partner(step, x, y, z, core, sign)

        def source(step):
            other = 1 - 2 * (step // 64)
            return torus_partner(step, x, y, z, core, -sign * other)

        return target, source
    me = dp * n_ctx + ctx

    def target(step):
        t = (me + step) % count
        return t // n_ctx, t % n_ctx

    def source(step):
        t = (me - step + count) % count
        return t // n_ctx, t % n_ctx

    return target, source


def layer_kernel(
    n_dp,
    n_ctx,
    group,
    ids,
    raw,
    queries,
    keys,
    values,
    out_grad,
    gate_hbm,
    up_hbm,
    down_hbm,
    moe_out,
    query_grad,
    key_grad,
    value_grad,
    score_grad,
    w_gate,
    w_up,
    w_down,
    grad_out,
    grad_in,
    row_out,
    row_in,
    back_rows,
    back_outs,
    canon_x,
    canon_g,
    halves,
    rank_et,
    mix_main,
    mix_spill,
    all_keys,
    all_values,
    key_dup,
    value_dup,
    key_dup_t,
    value_dup_t,
    bias,
    attn,
    log_total,
    wide,
    pick_et,
    key_acc,
    value_acc,
    pair_part,
    pair_in,
    w_sem,
    kv_send,
    kv_recv,
    g_send,
    g_recv,
    x_send,
    x_recv,
    r_send,
    r_recv,
    y_send,
    y_recv,
    p_send,
    p_recv,
):
    count = n_dp * n_ctx
    groups = count // group
    tokens = queries.shape[0]
    width = queries.shape[1]
    pairs = width // PAIR
    per_kv = pairs // 2
    length = n_ctx * tokens
    dp, ctx = lax.axis_index("dp"), lax.axis_index("ctx")
    me = dp * n_ctx + ctx
    target, source = partners(n_dp, n_ctx)
    neighbour = target(1)

    weight_copies = [
        pltpu.make_async_copy(src, dst, w_sem.at[n])
        for n, (src, dst) in enumerate(((gate_hbm, w_gate), (up_hbm, w_up), (down_hbm, w_down)))
    ]
    for copy in weight_copies:
        copy.start()

    barrier = pltpu.get_barrier_semaphore()

    def greet(step, carry):
        pl.semaphore_signal(barrier, inc=1, device_id=target(step), device_id_type=MESH)
        return carry

    lax.fori_loop(1, count, greet, 0)

    expert_row = iota((count, tokens), 0)
    scores_t = raw[...]
    total_t = jnp.sum(scores_t, axis=0, keepdims=True)
    mixing_t = scores_t / total_t
    named = jnp.zeros((count, tokens), F32)
    mix_et = jnp.zeros((count, tokens), F32)
    for k in range(ids.shape[0]):
        hit = expert_row == ids[k : k + 1, :]
        named = named + jnp.where(hit, 1.0, 0.0)
        mix_et = mix_et + jnp.where(hit, mixing_t[k : k + 1, :], 0.0)
    before = jnp.where(iota((tokens, tokens), 0) < iota((tokens, tokens), 1), 1.0, 0.0)
    rank = dot(named.astype(BF16), before.astype(BF16))
    rank = jnp.where(named > 0.0, rank, -1.0)
    rank_et[...] = rank

    spread = jnp.where(
        iota((count, count * ROWS), 0) == iota((count, count * ROWS), 1) // ROWS, 1.0, 0.0
    ).astype(BF16)
    lane_row = iota((tokens, count * ROWS), 1) % ROWS
    rank_wide = dot(rank.T.astype(BF16), spread)
    mix_wide = dot(mix_et.T.astype(BF16), spread)
    slot_main = (lane_row % 8).astype(F32)
    slot_spill = (8 + lane_row % 2).astype(F32)
    main_mix = jnp.where(rank_wide == slot_main, mix_wide, 0.0)
    mix_main[0:tokens, :] = jnp.where(lane_row < 8, main_mix, 0.0).astype(BF16)
    mix_main[tokens:, :] = jnp.where(lane_row >= 8, main_mix, 0.0).astype(BF16)
    mix_spill[...] = jnp.where(rank_wide == slot_spill, mix_wide, 0.0).astype(BF16)

    p_out, p_in = iota((256, 256), 0), iota((256, 256), 1)
    to_blocks = jnp.where(
        (p_out // 32 == (p_in % 16) // 2)
        & ((p_out % 32) // 2 == p_in // 16)
        & (p_out % 2 == p_in % 2),
        1.0,
        0.0,
    ).astype(BF16)
    to_chunks = jnp.where(
        (p_in // 32 == (p_out % 16) // 2)
        & ((p_in % 32) // 2 == p_out // 16)
        & (p_out % 2 == p_in % 2),
        1.0,
        0.0,
    ).astype(BF16)
    repeat_main = jnp.where(iota((256, BLOCK), 0) // ROWS == iota((256, BLOCK), 1), 1.0, 0.0).astype(BF16)
    repeat_spill = jnp.where(iota((32, BLOCK), 0) // 2 == iota((32, BLOCK), 1), 1.0, 0.0).astype(BF16)

    def ranks_of(block):
        rows = rank_et[pl.ds(pl.multiple_of(block * BLOCK, BLOCK), BLOCK), :]
        return rows.astype(BF16)

    def pack_rows(dst):
        def body(block, carry):
            ranks = ranks_of(block)
            wide_rank = dot(repeat_main, ranks)
            row = iota((256, tokens), 0) % ROWS
            hit = wide_rank == (row % 8).astype(F32)
            left = jnp.where(hit & (row < 8), 1.0, 0.0).astype(BF16)
            right = jnp.where(hit & (row >= 8), 1.0, 0.0).astype(BF16)
            first = pl.ds(pl.multiple_of(block * BLOCK, BLOCK), BLOCK)
            main = dot(jnp.concatenate([left, right], axis=1), halves[...])
            dst[first, :, 0:MAIN] = main.astype(BF16).reshape(BLOCK, ROWS, MAIN)
            spill_rank = dot(repeat_spill, ranks)
            spill_slot = (8 + iota((32, tokens), 0) % 2).astype(F32)
            spill_hit = jnp.where(spill_rank == spill_slot, 1.0, 0.0).astype(BF16)
            rows = [
                dot(spill_hit, halves[0:tokens, :]).astype(BF16),
                dot(spill_hit, halves[tokens:, :]).astype(BF16),
            ]
            dst[first, :, MAIN:] = spill_to_chunk(rows)
            return carry

        lax.fori_loop(0, count // BLOCK, body, 0)

    def spill_to_chunk(rows):
        stacked = jnp.concatenate(
            [part[:, c * SPILL : (c + 1) * SPILL] for part in rows for c in range(4)], axis=0
        )
        return dot(to_chunks, stacked).astype(BF16).reshape(BLOCK, ROWS, SPILL)

    def send_out(src, dst, send_sem, recv_sem):
        own = pltpu.make_async_copy(src.at[me], dst.at[0], recv_sem.at[0])
        own.start()

        def body(step, carry):
            tdp, tctx = target(step)
            pltpu.make_async_remote_copy(
                src_ref=src.at[tdp * n_ctx + tctx],
                dst_ref=dst.at[step],
                send_sem=send_sem,
                recv_sem=recv_sem.at[step // group],
                device_id=(tdp, tctx),
                device_id_type=MESH,
            ).start()
            return carry

        lax.fori_loop(1, count, body, 0)

    def send_back(src, dst, send_sem, recv_sem, lo, hi):
        def body(step, carry):
            pltpu.make_async_remote_copy(
                src_ref=src.at[step],
                dst_ref=dst.at[me],
                send_sem=send_sem,
                recv_sem=recv_sem,
                device_id=source(step),
                device_id_type=MESH,
            ).start()
            return carry

        lax.fori_loop(lo, hi, body, 0)

    def bytes_of(ref, amount, sem_a, sem_b):
        part = ref.at[pl.ds(0, amount)]
        return pltpu.make_async_remote_copy(
            src_ref=part,
            dst_ref=part,
            send_sem=sem_a,
            recv_sem=sem_b,
            device_id=neighbour,
            device_id_type=MESH,
        )

    halves[0:tokens, :] = out_grad[:, 0:MAIN]
    halves[tokens:, :] = out_grad[:, MAIN:]
    pack_rows(grad_out)

    pl.semaphore_wait(barrier, count - 1)
    here = pl.ds(pl.multiple_of(ctx * tokens, tokens), tokens)
    all_keys[here, :] = keys[...]
    all_values[here, :] = values[...]

    def send_pair(j, carry):
        peer = (dp, (ctx + j) % n_ctx)
        for n, (src, dst) in enumerate(((keys, all_keys), (values, all_values))):
            pltpu.make_async_remote_copy(
                src_ref=src,
                dst_ref=dst.at[here],
                send_sem=kv_send.at[n],
                recv_sem=kv_recv.at[n],
                device_id=peer,
                device_id_type=MESH,
            ).start()
        return carry

    lax.fori_loop(1, n_ctx, send_pair, 0)
    send_out(grad_out, grad_in, g_send, g_recv)

    key_at = iota((length, 2 * tokens), 0)
    query_at = ctx * tokens + iota((length, 2 * tokens), 1) % tokens
    bias[...] = jnp.where(key_at <= query_at, 0.0, NEGATIVE)
    for n, ref in enumerate((all_keys, all_values)):
        pair_wait = bytes_of(ref, (n_ctx - 1) * tokens, kv_send.at[n], kv_recv.at[n])
        pair_wait.wait()
    for g in range(2):
        select = jnp.where(
            iota((PAIR, PAIR), 0) == g * HD + iota((PAIR, PAIR), 1) % HD, 1.0, 0.0
        ).astype(BF16)
        select_t = jnp.where(
            iota((PAIR, PAIR), 1) == g * HD + iota((PAIR, PAIR), 0) % HD, 1.0, 0.0
        ).astype(BF16)
        key_dup[g] = dot(all_keys[...], select).astype(BF16)
        value_dup[g] = dot(all_values[...], select).astype(BF16)
        key_dup_t[g] = dot_nt(select_t, all_keys[...]).astype(BF16)
        value_dup_t[g] = dot_nt(select_t, all_values[...]).astype(BF16)

    low = iota((tokens, PAIR), 1) < HD

    def two_heads(rows):
        return jnp.concatenate(
            [jnp.where(low, rows, 0.0), jnp.where(low, 0.0, rows)], axis=0
        ).astype(BF16)

    def join_heads(both_t):
        both = both_t.T
        return jnp.where(low, both[0:tokens], both[tokens:])

    def columns(p):
        return pl.ds(pl.multiple_of(p * PAIR, PAIR), PAIR)

    scale = HD**-0.5

    def forward(p, carry):
        g = p // per_kv
        query = two_heads(queries[:, columns(p)].astype(F32) * scale)
        scores = dot_nt(key_dup[g], query) + bias[...]
        top = jnp.max(scores, axis=0, keepdims=True)
        weights = jnp.exp(scores - top)
        total = jnp.sum(weights, axis=0, keepdims=True)
        out_t = dot(value_dup_t[g], weights.astype(BF16)) / total
        attn[:, columns(p)] = join_heads(out_t).astype(BF16)
        log_total[p] = top + jnp.log(total)
        return carry

    lax.fori_loop(0, pairs, forward, 0)

    attn_wide = attn[...].astype(F32)
    inv_rms = lax.rsqrt(jnp.mean(attn_wide * attn_wide, axis=1, keepdims=True) + EPSILON)
    normed = (attn_wide * inv_rms).astype(BF16)
    halves[0:tokens, :] = normed[:, 0:MAIN]
    halves[tokens:, :] = normed[:, MAIN:]
    pack_rows(row_out)
    send_out(row_out, row_in, x_send, x_recv)
    for copy in weight_copies:
        copy.wait()

    main_rows = group * 8

    def unpack(buf, start, canon):
        def body(j, carry):
            both = buf[pl.ds(start + 2 * j, 2), :, 0:MAIN].astype(F32)
            at = pl.ds(pl.multiple_of(j * 16, 16), 16)
            for h in range(2):
                part = jnp.concatenate(
                    [both[0, 8 * h : 8 * h + 8], both[1, 8 * h : 8 * h + 8]], axis=0
                )
                canon[at, h * MAIN : (h + 1) * MAIN] = part.astype(BF16)
            return carry

        lax.fori_loop(0, group // 2, body, 0)
        for b in range(group // BLOCK):
            spill = buf[pl.ds(start + b * BLOCK, BLOCK), :, MAIN:].reshape(256, SPILL)
            moved = dot(to_blocks, spill).astype(BF16)
            for c in range(8):
                canon[
                    main_rows + 32 * b : main_rows + 32 * (b + 1), c * SPILL : (c + 1) * SPILL
                ] = moved[32 * c : 32 * (c + 1)]

    def repack(canon, buf, start):
        def body(j, carry):
            both = canon[pl.ds(pl.multiple_of(j * 16, 16), 16), :].astype(F32)
            for s in range(2):
                part = jnp.concatenate(
                    [both[8 * s : 8 * s + 8, 0:MAIN], both[8 * s : 8 * s + 8, MAIN:]], axis=0
                )
                buf[start + 2 * j + s, :, 0:MAIN] = part.astype(BF16)
            return carry

        lax.fori_loop(0, group // 2, body, 0)
        for b in range(group // BLOCK):
            rows = canon[main_rows + 32 * b : main_rows + 32 * (b + 1), :]
            buf[pl.ds(start + b * BLOCK, BLOCK), :, MAIN:] = spill_to_chunk(
                [rows[:, 0:MAIN], rows[:, MAIN:]]
            )

    def expert(n, carry):
        start = n * group
        bytes_of(grad_in, group, g_send, g_recv.at[n]).wait_recv()
        bytes_of(row_in, group, x_send, x_recv.at[n]).wait_recv()
        unpack(row_in, start, canon_x)
        unpack(grad_in, start, canon_g)
        gate_act = dot(canon_x[...], w_gate[...])
        up_act = dot(canon_x[...], w_up[...])
        sigmoid = jax.nn.sigmoid(gate_act)
        silu = gate_act * sigmoid
        hidden = (silu * up_act).astype(BF16)
        hidden_grad = dot_nt(canon_g[...], w_down[...])
        gate_grad = (hidden_grad * up_act * sigmoid * (1.0 + gate_act * (1.0 - sigmoid))).astype(BF16)
        up_grad = (hidden_grad * silu).astype(BF16)
        canon_x[...] = (dot_nt(gate_grad, w_gate[...]) + dot_nt(up_grad, w_up[...])).astype(BF16)
        repack(canon_x, row_in, start)
        send_back(row_in, back_rows, r_send, r_recv, jnp.maximum(start, 1), start + group)
        canon_g[...] = dot(hidden, w_down[...]).astype(BF16)
        repack(canon_g, grad_in, start)
        return carry

    lax.fori_loop(0, groups, expert, 0)
    pltpu.make_async_copy(row_in.at[0], back_rows.at[me], r_recv).start()
    pltpu.make_async_copy(grad_in.at[0], back_outs.at[me], y_recv).start()
    send_back(grad_in, back_outs, y_send, y_recv, 1, count)

    def combine(buf):
        for n in range(4):
            cols = slice(n * 256, (n + 1) * 256)
            part = dot(mix_main[...], buf[:, :, cols].reshape(count * ROWS, 256))
            wide[:, n * 256 : (n + 1) * 256] = part[0:tokens]
            wide[:, MAIN + n * 256 : MAIN + (n + 1) * 256] = part[tokens:]
        spill = buf[:, :, MAIN:].reshape(count * ROWS, SPILL)
        block_of = (iota((tokens, count * ROWS), 1) % ROWS) // 2
        for c in range(8):
            picked = jnp.where(block_of == c, mix_spill[...].astype(F32), 0.0).astype(BF16)
            wide[:, c * SPILL : (c + 1) * SPILL] += dot(picked, spill)

    bytes_of(back_rows, count, r_send, r_recv).wait_recv()
    combine(back_rows)
    normed_grad = wide[...]
    attn_again = attn[...].astype(F32)
    inv = lax.rsqrt(jnp.mean(attn_again * attn_again, axis=1, keepdims=True) + EPSILON)
    shared = jnp.mean(normed_grad * attn_again, axis=1, keepdims=True)
    wide[...] = inv * normed_grad - inv * inv * inv * attn_again * shared

    key_acc[...] = jnp.zeros_like(key_acc)
    value_acc[...] = jnp.zeros_like(value_acc)

    def backward(p, carry):
        g = p // per_kv
        query = two_heads(queries[:, columns(p)].astype(F32) * scale)
        grad = wide[:, columns(p)].astype(BF16).astype(F32)
        grads = two_heads(grad)
        product_t = (grad * attn[:, columns(p)].astype(F32)).T
        delta = jnp.concatenate(
            [
                jnp.sum(product_t[0:HD], axis=0, keepdims=True),
                jnp.sum(product_t[HD:], axis=0, keepdims=True),
            ],
            axis=1,
        )
        scores = dot_nt(key_dup[g], query) + bias[...]
        weights = jnp.exp(scores - log_total[p])
        prob_grad = dot_nt(value_dup[g], grads)
        score_grads = (weights * (prob_grad - delta)).astype(BF16)
        query_t = dot(key_dup_t[g], score_grads) * scale
        query_grad[:, columns(p)] = join_heads(query_t).astype(BF16)
        key_acc[g] += dot(score_grads, query)
        value_acc[g] += dot(weights.astype(BF16), grads)
        return carry

    lax.fori_loop(0, pairs, backward, 0)

    low_long = iota((length, PAIR), 1) < HD
    for n, acc in enumerate((key_acc, value_acc)):
        first = acc[0] + pltpu.roll(acc[0], HD, 1)
        second = acc[1] + pltpu.roll(acc[1], HD, 1)
        pair_part[:, n * PAIR : (n + 1) * PAIR] = jnp.where(low_long, first, second)

    def send_part(j, carry):
        peer = (ctx + j) % n_ctx
        pltpu.make_async_remote_copy(
            src_ref=pair_part.at[pl.ds(pl.multiple_of(peer * tokens, tokens), tokens)],
            dst_ref=pair_in.at[j],
            send_sem=p_send,
            recv_sem=p_recv,
            device_id=(dp, peer),
            device_id_type=MESH,
        ).start()
        return carry

    lax.fori_loop(1, n_ctx, send_part, 0)

    bytes_of(back_outs, count, y_send, y_recv).wait_recv()
    combine(back_outs)
    moe_out[...] = wide[...].astype(BF16)

    def weigh(block, carry):
        first = pl.ds(pl.multiple_of(block * BLOCK, BLOCK), BLOCK)
        sent = grad_out[first].reshape(256, CHUNK).astype(F32)
        got = back_outs[first].reshape(256, CHUNK).astype(F32)
        product = sent * got
        main = jnp.sum(product[:, 0:MAIN], axis=1, keepdims=True)
        spill = jnp.sum(product[:, MAIN:], axis=1, keepdims=True)
        ranks = dot(repeat_main, ranks_of(block))
        row = iota((256, tokens), 0) % ROWS
        found = jnp.where(ranks == (row % 8).astype(F32), main, 0.0) + jnp.where(
            ranks == (8 + row % 2).astype(F32), spill, 0.0
        )
        pick_et[first, :] = jnp.sum(found.reshape(BLOCK, ROWS, tokens), axis=1)
        return carry

    lax.fori_loop(0, count // BLOCK, weigh, 0)
    dots = pick_et[...]
    weight_grad = jnp.concatenate(
        [
            jnp.sum(
                jnp.where(iota((count, tokens), 0) == ids[k : k + 1, :], dots, 0.0),
                axis=0,
                keepdims=True,
            )
            for k in range(ids.shape[0])
        ],
        axis=0,
    )
    score_again = raw[...]
    sum_again = jnp.sum(score_again, axis=0, keepdims=True)
    mixing_again = score_again / sum_again
    score_grad[...] = (
        weight_grad - jnp.sum(mixing_again * weight_grad, axis=0, keepdims=True)
    ) / sum_again

    parts_wait = bytes_of(pair_in, n_ctx - 1, p_send, p_recv)
    parts_wait.wait()
    pair_sum = pair_part[here, :]
    for j in range(1, n_ctx):
        pair_sum = pair_sum + pair_in[j]
    key_grad[...] = pair_sum[:, 0:PAIR].astype(BF16)
    value_grad[...] = pair_sum[:, PAIR:].astype(BF16)

    for ref, sem_s, sem_r in (
        (grad_out, g_send, g_recv.at[0]),
        (row_out, x_send, x_recv.at[0]),
        (row_in, r_send, r_recv),
        (grad_in, y_send, y_recv),
    ):
        bytes_of(ref, count - 1, sem_s, sem_r).wait_send()


def shards(
    n_dp,
    n_ctx,
    queries,
    keys,
    values,
    expert_ids,
    router_scores,
    gate_weight,
    up_weight,
    down_weight,
    out_grad,
):
    count = n_dp * n_ctx
    group = max(BLOCK, count // 4)
    groups = count // group
    tokens, width = queries.shape[1:]
    pair_width = keys.shape[2]
    top = expert_ids.shape[2]
    hidden = gate_weight.shape[2]
    length = n_ctx * tokens
    pairs = width // PAIR
    chunk_buf = pltpu.VMEM((count, ROWS, CHUNK), BF16)
    dma = pltpu.SemaphoreType.DMA
    vmem = pl.BlockSpec(memory_space=pltpu.VMEM)
    hbm = pl.BlockSpec(memory_space=pl.ANY)
    canon = pltpu.VMEM((group * 10, width), BF16)
    outs = pl.pallas_call(
        functools.partial(layer_kernel, n_dp, n_ctx, group),
        out_shape=(
            jax.ShapeDtypeStruct((tokens, width), BF16),
            jax.ShapeDtypeStruct((tokens, width), BF16),
            jax.ShapeDtypeStruct((tokens, pair_width), BF16),
            jax.ShapeDtypeStruct((tokens, pair_width), BF16),
            jax.ShapeDtypeStruct((top, tokens), F32),
        ),
        in_specs=[vmem] * 6 + [hbm] * 3,
        out_specs=[vmem] * 5,
        scratch_shapes=[
            pltpu.VMEM((width, hidden), BF16),
            pltpu.VMEM((width, hidden), BF16),
            pltpu.VMEM((hidden, width), BF16),
            chunk_buf,
            chunk_buf,
            chunk_buf,
            chunk_buf,
            chunk_buf,
            chunk_buf,
            canon,
            canon,
            pltpu.VMEM((2 * tokens, MAIN), BF16),
            pltpu.VMEM((count, tokens), F32),
            pltpu.VMEM((2 * tokens, count * ROWS), BF16),
            pltpu.VMEM((tokens, count * ROWS), BF16),
            pltpu.VMEM((length, pair_width), BF16),
            pltpu.VMEM((length, pair_width), BF16),
            pltpu.VMEM((2, length, PAIR), BF16),
            pltpu.VMEM((2, length, PAIR), BF16),
            pltpu.VMEM((2, PAIR, length), BF16),
            pltpu.VMEM((2, PAIR, length), BF16),
            pltpu.VMEM((length, 2 * tokens), F32),
            pltpu.VMEM((tokens, width), BF16),
            pltpu.VMEM((pairs, 1, 2 * tokens), F32),
            pltpu.VMEM((tokens, width), F32),
            pltpu.VMEM((count, tokens), F32),
            pltpu.VMEM((2, length, PAIR), F32),
            pltpu.VMEM((2, length, PAIR), F32),
            pltpu.VMEM((length, 2 * PAIR), F32),
            pltpu.VMEM((n_ctx, tokens, 2 * PAIR), F32),
            dma((3,)),
            dma((2,)),
            dma((2,)),
            dma,
            dma((groups,)),
            dma,
            dma((groups,)),
            dma,
            dma,
            dma,
            dma,
            dma,
            dma,
        ],
        compiler_params=pltpu.CompilerParams(
            collective_id=0, has_side_effects=True, vmem_limit_bytes=63 * 2**20
        ),
        name="layer",
    )(
        expert_ids[0].T,
        router_scores[0].T,
        queries[0],
        keys[0],
        values[0],
        out_grad[0],
        gate_weight[0],
        up_weight[0],
        down_weight[0],
    )
    moe_out, query_grad, key_grad, value_grad, score_grad = outs
    return (
        moe_out[None],
        query_grad[None],
        key_grad[None],
        value_grad[None],
        score_grad.T[None],
    )


def solution(mesh):
    split = P("dp", "ctx", None)
    whole = P(("dp", "ctx"), None, None)
    return jax.shard_map(
        functools.partial(shards, mesh.shape["dp"], mesh.shape["ctx"]),
        mesh=mesh,
        in_specs=(split, split, split, split, split, whole, whole, whole, split),
        out_specs=(split,) * 5,
        check_vma=False,
    )
```

time: 714 us -> 314 us (0.44)
  the two profiles are of different devices: /device:TPU:0 before, /device:TPU:3 now
where the time goes in v2:
time: 314 us
  Pallas kernels  305 us (97%)
  local copies, waits for them, and re-layouts  7.79 us (2%)
    pallas_call x1, Pallas kernels, shards(): pl.pallas_call(functools.partial(layer_kernel, n_dp, n_ctx, group), out_s...  305 us
    unnamed x5, local copies, waits for them, and re-layouts  7.79 us

profile of v2, /device:TPU:3, one launch (start us, length us, event | category | flops | bytes accessed | tf_op | source)
XLA Modules:
  0.0 313.9 jit_solution(8266750183136416633)
XLA Ops:
  0.6 305.4 %layer.1 = (bf16[128,2048]{1,0:T(8,128)(2,1)}, bf16[128,2048]{1,0:T(8,128)(2,1)}, bf16[128,128]{1,0:T(8,128)(2,1)}, bf16[128,128]{1,0:T(8,128)(2,1)}, f32[8,128]{1,0:T(8,128)}) custom-call(s32[8,128]{1,0:T(8,128)} %bitcast.31, f32[8,128]{1,0:T(8,128)} %bitcast.32, bf16[128,2048]{1,0:T(8,128)(2,1)} %bitcast.23, bf16[128,128]{1,0:T(8,128)(2,1)} %bitcast.27, ...), custom_call_target="tpu_custom_call" | custom-call | tf_op jit(solution)/shard_map/layer/pallas_call | solution.py:589
  306.1 1.9 copy.19
  307.9 1.9 copy.20
  309.8 1.4 copy.21
  311.2 1.4 copy.22
  312.6 1.3 copy.23

commit v3 on v2

--- a/solution.py
+++ b/solution.py
@@ -34,17 +34,25 @@
     return lax.broadcasted_iota(jnp.int32, shape, dim)
 
 
+def quo(a, n):
+    return lax.shift_right_logical(a, jnp.int32(n.bit_length() - 1)) if a.ndim else a // n
+
+
+def rem(a, n):
+    return jnp.bitwise_and(a, n - 1) if a.ndim else a % n
+
+
 def torus_partner(step, x, y, z, core, sign):
-    inner = step % 64
-    a, b, c = inner // 16, (inner // 4) % 4, inner % 4
+    inner = rem(step, 64)
+    a, b, c = quo(inner, 16), rem(quo(inner, 4), 4), rem(inner, 4)
     dx = c
-    dy = (c + b) % 4
-    dz = (c + a + 2 * b) % 4
-    tx = (x + sign * dx + 4) % 4
-    ty = (y + sign * dy + 4) % 4
-    tz = (z + sign * dz + 4) % 4
-    tcore = (core + step // 64) % 2
-    return tx * 4 + (tz % 2) * 2 + tcore, ty * 2 + tz // 2
+    dy = rem(c + b, 4)
+    dz = rem(c + a + 2 * b, 4)
+    tx = rem(x + sign * dx + 4, 4)
+    ty = rem(y + sign * dy + 4, 4)
+    tz = rem(z + sign * dz + 4, 4)
+    tcore = rem(core + quo(step, 64), 2)
+    return tx * 4 + rem(tz, 2) * 2 + tcore, ty * 2 + quo(tz, 2)
 
 
 def partners(n_dp, n_ctx):
@@ -56,9 +64,11 @@
         sign = 1 - 2 * core
 
         def target(step):
+            step = jnp.asarray(step, jnp.int32)
             return torus_partner(step, x, y, z, core, sign)
 
         def source(step):
+            step = jnp.asarray(step, jnp.int32)
             other = 1 - 2 * (step // 64)
             return torus_partner(step, x, y, z, core, -sign * other)
 
@@ -66,8 +76,9 @@
     me = dp * n_ctx + ctx
 
     def target(step):
-        t = (me + step) % count
-        return t // n_ctx, t % n_ctx
+        step = jnp.asarray(step, jnp.int32)
+        t = rem(me + step, count)
+        return quo(t, n_ctx), rem(t, n_ctx)
 
     def source(step):
         t = (me - step + count) % count
@@ -154,8 +165,8 @@
         pltpu.make_async_copy(src, dst, w_sem.at[n])
         for n, (src, dst) in enumerate(((gate_hbm, w_gate), (up_hbm, w_up), (down_hbm, w_down)))
     ]
-    for copy in weight_copies:
-        copy.start()
+    all_keys[...] = jnp.zeros_like(all_keys)
+    all_values[...] = jnp.zeros_like(all_values)
 
     barrier = pltpu.get_barrier_semaphore()
 
@@ -165,78 +176,60 @@
 
     lax.fori_loop(1, count, greet, 0)
 
-    expert_row = iota((count, tokens), 0)
-    scores_t = raw[...]
-    total_t = jnp.sum(scores_t, axis=0, keepdims=True)
-    mixing_t = scores_t / total_t
+    tdp_row, tctx_row = target(iota((count, tokens), 0))
+    expert_row = (tdp_row * n_ctx + tctx_row).astype(F32)
+    ids_t = ids[...].astype(F32)
     named = jnp.zeros((count, tokens), F32)
-    mix_et = jnp.zeros((count, tokens), F32)
-    for k in range(ids.shape[0]):
-        hit = expert_row == ids[k : k + 1, :]
-        named = named + jnp.where(hit, 1.0, 0.0)
-        mix_et = mix_et + jnp.where(hit, mixing_t[k : k + 1, :], 0.0)
+    for k in range(ids_t.shape[0]):
+        named = named + jnp.where(expert_row == ids_t[k : k + 1, :], 1.0, 0.0)
     before = jnp.where(iota((tokens, tokens), 0) < iota((tokens, tokens), 1), 1.0, 0.0)
     rank = dot(named.astype(BF16), before.astype(BF16))
-    rank = jnp.where(named > 0.0, rank, -1.0)
-    rank_et[...] = rank
-
-    spread = jnp.where(
-        iota((count, count * ROWS), 0) == iota((count, count * ROWS), 1) // ROWS, 1.0, 0.0
-    ).astype(BF16)
-    lane_row = iota((tokens, count * ROWS), 1) % ROWS
-    rank_wide = dot(rank.T.astype(BF16), spread)
-    mix_wide = dot(mix_et.T.astype(BF16), spread)
-    slot_main = (lane_row % 8).astype(F32)
-    slot_spill = (8 + lane_row % 2).astype(F32)
-    main_mix = jnp.where(rank_wide == slot_main, mix_wide, 0.0)
-    mix_main[0:tokens, :] = jnp.where(lane_row < 8, main_mix, 0.0).astype(BF16)
-    mix_main[tokens:, :] = jnp.where(lane_row >= 8, main_mix, 0.0).astype(BF16)
-    mix_spill[...] = jnp.where(rank_wide == slot_spill, mix_wide, 0.0).astype(BF16)
+    rank_et[...] = jnp.where(named > 0.0, rank, -1.0)
 
     p_out, p_in = iota((256, 256), 0), iota((256, 256), 1)
     to_blocks = jnp.where(
-        (p_out // 32 == (p_in % 16) // 2)
-        & ((p_out % 32) // 2 == p_in // 16)
-        & (p_out % 2 == p_in % 2),
+        (quo(p_out, 32) == quo(rem(p_in, 16), 2))
+        & (quo(rem(p_out, 32), 2) == quo(p_in, 16))
+        & (rem(p_out, 2) == rem(p_in, 2)),
         1.0,
         0.0,
     ).astype(BF16)
     to_chunks = jnp.where(
-        (p_in // 32 == (p_out % 16) // 2)
-        & ((p_in % 32) // 2 == p_out // 16)
-        & (p_out % 2 == p_in % 2),
+        (quo(p_in, 32) == quo(rem(p_out, 16), 2))
+        & (quo(rem(p_in, 32), 2) == quo(p_out, 16))
+        & (rem(p_out, 2) == rem(p_in, 2)),
         1.0,
         0.0,
     ).astype(BF16)
-    repeat_main = jnp.where(iota((256, BLOCK), 0) // ROWS == iota((256, BLOCK), 1), 1.0, 0.0).astype(BF16)
-    repeat_spill = jnp.where(iota((32, BLOCK), 0) // 2 == iota((32, BLOCK), 1), 1.0, 0.0).astype(BF16)
+    repeat_main = jnp.where(
+        quo(iota((256, BLOCK), 0), ROWS) == iota((256, BLOCK), 1), 1.0, 0.0
+    ).astype(BF16)
+    repeat_spill = jnp.where(quo(iota((32, BLOCK), 0), 2) == iota((32, BLOCK), 1), 1.0, 0.0).astype(
+        BF16
+    )
+    block_row = rem(iota((256, tokens), 0), ROWS)
+    main_slot = rem(block_row, 8).astype(F32)
+    spill_slot = (8 + rem(block_row, 2)).astype(F32)
+    spill_row_slot = (8 + rem(iota((32, tokens), 0), 2)).astype(F32)
 
     def ranks_of(block):
         rows = rank_et[pl.ds(pl.multiple_of(block * BLOCK, BLOCK), BLOCK), :]
         return rows.astype(BF16)
 
-    def pack_rows(dst):
-        def body(block, carry):
-            ranks = ranks_of(block)
-            wide_rank = dot(repeat_main, ranks)
-            row = iota((256, tokens), 0) % ROWS
-            hit = wide_rank == (row % 8).astype(F32)
-            left = jnp.where(hit & (row < 8), 1.0, 0.0).astype(BF16)
-            right = jnp.where(hit & (row >= 8), 1.0, 0.0).astype(BF16)
-            first = pl.ds(pl.multiple_of(block * BLOCK, BLOCK), BLOCK)
-            main = dot(jnp.concatenate([left, right], axis=1), halves[...])
-            dst[first, :, 0:MAIN] = main.astype(BF16).reshape(BLOCK, ROWS, MAIN)
-            spill_rank = dot(repeat_spill, ranks)
-            spill_slot = (8 + iota((32, tokens), 0) % 2).astype(F32)
-            spill_hit = jnp.where(spill_rank == spill_slot, 1.0, 0.0).astype(BF16)
-            rows = [
-                dot(spill_hit, halves[0:tokens, :]).astype(BF16),
-                dot(spill_hit, halves[tokens:, :]).astype(BF16),
-            ]
-            dst[first, :, MAIN:] = spill_to_chunk(rows)
-            return carry
-
-        lax.fori_loop(0, count // BLOCK, body, 0)
+    def pack_block(dst, block):
+        ranks = ranks_of(block)
+        hit = dot(repeat_main, ranks) == main_slot
+        left = jnp.where(hit & (block_row < 8), 1.0, 0.0).astype(BF16)
+        right = jnp.where(hit & (block_row >= 8), 1.0, 0.0).astype(BF16)
+        first = pl.ds(pl.multiple_of(block * BLOCK, BLOCK), BLOCK)
+        main = dot(jnp.concatenate([left, right], axis=1), halves[...])
+        dst[first, :, 0:MAIN] = main.astype(BF16).reshape(BLOCK, ROWS, MAIN)
+        spill_hit = jnp.where(dot(repeat_spill, ranks) == spill_row_slot, 1.0, 0.0).astype(BF16)
+        rows = [
+            dot(spill_hit, halves[0:tokens, :]).astype(BF16),
+            dot(spill_hit, halves[tokens:, :]).astype(BF16),
+        ]
+        dst[first, :, MAIN:] = spill_to_chunk(rows)
 
     def spill_to_chunk(rows):
         stacked = jnp.concatenate(
@@ -245,30 +238,32 @@
         return dot(to_chunks, stacked).astype(BF16).reshape(BLOCK, ROWS, SPILL)
 
     def send_out(src, dst, send_sem, recv_sem):
-        own = pltpu.make_async_copy(src.at[me], dst.at[0], recv_sem.at[0])
-        own.start()
-
-        def body(step, carry):
-            tdp, tctx = target(step)
+        def send(step, carry):
             pltpu.make_async_remote_copy(
-                src_ref=src.at[tdp * n_ctx + tctx],
+                src_ref=src.at[step],
                 dst_ref=dst.at[step],
                 send_sem=send_sem,
                 recv_sem=recv_sem.at[step // group],
-                device_id=(tdp, tctx),
+                device_id=target(step),
                 device_id_type=MESH,
             ).start()
             return carry
 
-        lax.fori_loop(1, count, body, 0)
+        def body(block, carry):
+            pack_block(src, block)
+            lax.fori_loop(jnp.maximum(block * BLOCK, 1), (block + 1) * BLOCK, send, 0)
+            return carry
+
+        lax.fori_loop(0, count // BLOCK, body, 0)
+        pltpu.make_async_copy(src.at[0], dst.at[0], recv_sem.at[0]).start()
 
     def send_back(src, dst, send_sem, recv_sem, lo, hi):
         def body(step, carry):
             pltpu.make_async_remote_copy(
                 src_ref=src.at[step],
-                dst_ref=dst.at[me],
+                dst_ref=dst.at[step],
                 send_sem=send_sem,
-                recv_sem=recv_sem,
+                recv_sem=recv_sem.at[step // group],
                 device_id=source(step),
                 device_id_type=MESH,
             ).start()
@@ -287,43 +282,50 @@
             device_id_type=MESH,
         )
 
+    pl.semaphore_wait(barrier, count - 1)
+    here = pl.ds(pl.multiple_of(ctx * tokens, tokens), tokens)
+    pair_copies = ((keys, all_keys), (values, all_values))
+
+    def pair_copy(n, peer, at):
+        return pltpu.make_async_remote_copy(
+            src_ref=pair_copies[n][0],
+            dst_ref=pair_copies[n][1].at[pl.ds(pl.multiple_of(at * tokens, tokens), tokens)],
+            send_sem=kv_send.at[n, peer],
+            recv_sem=kv_recv.at[n, at],
+            device_id=(dp, peer),
+            device_id_type=MESH,
+        )
+
+    def send_pair(peer, carry):
+        for n in range(2):
+            pair_copy(n, peer, ctx).start()
+        return carry
+
+    lax.fori_loop(ctx + 1, n_ctx, send_pair, 0)
     halves[0:tokens, :] = out_grad[:, 0:MAIN]
     halves[tokens:, :] = out_grad[:, MAIN:]
-    pack_rows(grad_out)
-
-    pl.semaphore_wait(barrier, count - 1)
-    here = pl.ds(pl.multiple_of(ctx * tokens, tokens), tokens)
+    send_out(grad_out, grad_in, g_send, g_recv)
+    for copy in weight_copies:
+        copy.start()
+
     all_keys[here, :] = keys[...]
     all_values[here, :] = values[...]
-
-    def send_pair(j, carry):
-        peer = (dp, (ctx + j) % n_ctx)
-        for n, (src, dst) in enumerate(((keys, all_keys), (values, all_values))):
-            pltpu.make_async_remote_copy(
-                src_ref=src,
-                dst_ref=dst.at[here],
-                send_sem=kv_send.at[n],
-                recv_sem=kv_recv.at[n],
-                device_id=peer,
-                device_id_type=MESH,
-            ).start()
-        return carry
-
-    lax.fori_loop(1, n_ctx, send_pair, 0)
-    send_out(grad_out, grad_in, g_send, g_recv)
-
     key_at = iota((length, 2 * tokens), 0)
-    query_at = ctx * tokens + iota((length, 2 * tokens), 1) % tokens
+    query_at = ctx * tokens + rem(iota((length, 2 * tokens), 1), tokens)
     bias[...] = jnp.where(key_at <= query_at, 0.0, NEGATIVE)
-    for n, ref in enumerate((all_keys, all_values)):
-        pair_wait = bytes_of(ref, (n_ctx - 1) * tokens, kv_send.at[n], kv_recv.at[n])
-        pair_wait.wait()
+
+    def wait_pair(at, carry):
+        for n in range(2):
+            pair_copy(n, at, at).wait_recv()
+        return carry
+
+    lax.fori_loop(0, ctx, wait_pair, 0)
     for g in range(2):
         select = jnp.where(
-            iota((PAIR, PAIR), 0) == g * HD + iota((PAIR, PAIR), 1) % HD, 1.0, 0.0
+            iota((PAIR, PAIR), 0) == g * HD + rem(iota((PAIR, PAIR), 1), HD), 1.0, 0.0
         ).astype(BF16)
         select_t = jnp.where(
-            iota((PAIR, PAIR), 1) == g * HD + iota((PAIR, PAIR), 0) % HD, 1.0, 0.0
+            iota((PAIR, PAIR), 1) == g * HD + rem(iota((PAIR, PAIR), 0), HD), 1.0, 0.0
         ).astype(BF16)
         key_dup[g] = dot(all_keys[...], select).astype(BF16)
         value_dup[g] = dot(all_values[...], select).astype(BF16)
@@ -365,8 +367,24 @@
     normed = (attn_wide * inv_rms).astype(BF16)
     halves[0:tokens, :] = normed[:, 0:MAIN]
     halves[tokens:, :] = normed[:, MAIN:]
-    pack_rows(row_out)
     send_out(row_out, row_in, x_send, x_recv)
+
+    scores_t = raw[...]
+    total_t = jnp.sum(scores_t, axis=0, keepdims=True)
+    mixing_t = scores_t / total_t
+    mix_et = jnp.zeros((count, tokens), F32)
+    for k in range(ids_t.shape[0]):
+        mix_et = mix_et + jnp.where(expert_row == ids_t[k : k + 1, :], mixing_t[k : k + 1, :], 0.0)
+    wide_shape = (count, count * ROWS)
+    spread = jnp.where(iota(wide_shape, 0) == quo(iota(wide_shape, 1), ROWS), 1.0, 0.0).astype(BF16)
+    lane_row = rem(iota((tokens, count * ROWS), 1), ROWS)
+    rank_wide = dot(rank_et[...].T.astype(BF16), spread)
+    mix_wide = dot(mix_et.T.astype(BF16), spread)
+    main_mix = jnp.where(rank_wide == rem(lane_row, 8).astype(F32), mix_wide, 0.0)
+    mix_main[0:tokens, :] = jnp.where(lane_row < 8, main_mix, 0.0).astype(BF16)
+    mix_main[tokens:, :] = jnp.where(lane_row >= 8, main_mix, 0.0).astype(BF16)
+    spill_mix = jnp.where(rank_wide == (8 + rem(lane_row, 2)).astype(F32), mix_wide, 0.0)
+    mix_spill[...] = spill_mix.astype(BF16)
     for copy in weight_copies:
         copy.wait()
 
@@ -431,24 +449,33 @@
         return carry
 
     lax.fori_loop(0, groups, expert, 0)
-    pltpu.make_async_copy(row_in.at[0], back_rows.at[me], r_recv).start()
-    pltpu.make_async_copy(grad_in.at[0], back_outs.at[me], y_recv).start()
+    pltpu.make_async_copy(row_in.at[0], back_rows.at[0], r_recv.at[0]).start()
+    pltpu.make_async_copy(grad_in.at[0], back_outs.at[0], y_recv.at[0]).start()
     send_back(grad_in, back_outs, y_send, y_recv, 1, count)
 
-    def combine(buf):
-        for n in range(4):
-            cols = slice(n * 256, (n + 1) * 256)
-            part = dot(mix_main[...], buf[:, :, cols].reshape(count * ROWS, 256))
-            wide[:, n * 256 : (n + 1) * 256] = part[0:tokens]
-            wide[:, MAIN + n * 256 : MAIN + (n + 1) * 256] = part[tokens:]
-        spill = buf[:, :, MAIN:].reshape(count * ROWS, SPILL)
-        block_of = (iota((tokens, count * ROWS), 1) % ROWS) // 2
+    def combine(buf, n):
+        mine = pl.ds(pl.multiple_of(n * group, group), group)
+        lanes = pl.ds(pl.multiple_of(n * group * ROWS, group * ROWS), group * ROWS)
+        for c in range(4):
+            rows = buf[mine, :, c * 256 : (c + 1) * 256].reshape(group * ROWS, 256)
+            part = dot(mix_main[:, lanes], rows)
+            wide[:, c * 256 : (c + 1) * 256] += part[0:tokens]
+            wide[:, MAIN + c * 256 : MAIN + (c + 1) * 256] += part[tokens:]
+        spill = buf[mine, :, MAIN:].reshape(group * ROWS, SPILL)
+        spill_mix = mix_spill[:, lanes].astype(F32)
+        column_block = quo(rem(iota((tokens, group * ROWS), 1), ROWS), 2)
         for c in range(8):
-            picked = jnp.where(block_of == c, mix_spill[...].astype(F32), 0.0).astype(BF16)
+            picked = jnp.where(column_block == c, spill_mix, 0.0).astype(BF16)
             wide[:, c * SPILL : (c + 1) * SPILL] += dot(picked, spill)
 
-    bytes_of(back_rows, count, r_send, r_recv).wait_recv()
-    combine(back_rows)
+    wide[...] = jnp.zeros_like(wide)
+
+    def take_rows(n, carry):
+        bytes_of(back_rows, group, r_send, r_recv.at[n]).wait_recv()
+        combine(back_rows, n)
+        return carry
+
+    lax.fori_loop(0, groups, take_rows, 0)
     normed_grad = wide[...]
     attn_again = attn[...].astype(F32)
     inv = lax.rsqrt(jnp.mean(attn_again * attn_again, axis=1, keepdims=True) + EPSILON)
@@ -487,27 +514,27 @@
     for n, acc in enumerate((key_acc, value_acc)):
         first = acc[0] + pltpu.roll(acc[0], HD, 1)
         second = acc[1] + pltpu.roll(acc[1], HD, 1)
-        pair_part[:, n * PAIR : (n + 1) * PAIR] = jnp.where(low_long, first, second)
-
-    def send_part(j, carry):
-        peer = (ctx + j) % n_ctx
-        pltpu.make_async_remote_copy(
+        pair_part[:, n * PAIR : (n + 1) * PAIR] = jnp.where(low_long, first, second).astype(BF16)
+
+    def part_copy(peer, distance):
+        return pltpu.make_async_remote_copy(
             src_ref=pair_part.at[pl.ds(pl.multiple_of(peer * tokens, tokens), tokens)],
-            dst_ref=pair_in.at[j],
-            send_sem=p_send,
-            recv_sem=p_recv,
+            dst_ref=pair_in.at[distance],
+            send_sem=p_send.at[distance],
+            recv_sem=p_recv.at[distance],
             device_id=(dp, peer),
             device_id_type=MESH,
-        ).start()
-        return carry
-
-    lax.fori_loop(1, n_ctx, send_part, 0)
-
-    bytes_of(back_outs, count, y_send, y_recv).wait_recv()
-    combine(back_outs)
-    moe_out[...] = wide[...].astype(BF16)
-
-    def weigh(block, carry):
+        )
+
+    def send_part(peer, carry):
+        part_copy(peer, ctx - peer).start()
+        return carry
+
+    lax.fori_loop(0, ctx, send_part, 0)
+
+    wide[...] = jnp.zeros_like(wide)
+
+    def weigh(block):
         first = pl.ds(pl.multiple_of(block * BLOCK, BLOCK), BLOCK)
         sent = grad_out[first].reshape(256, CHUNK).astype(F32)
         got = back_outs[first].reshape(256, CHUNK).astype(F32)
@@ -515,48 +542,86 @@
         main = jnp.sum(product[:, 0:MAIN], axis=1, keepdims=True)
         spill = jnp.sum(product[:, MAIN:], axis=1, keepdims=True)
         ranks = dot(repeat_main, ranks_of(block))
-        row = iota((256, tokens), 0) % ROWS
-        found = jnp.where(ranks == (row % 8).astype(F32), main, 0.0) + jnp.where(
-            ranks == (8 + row % 2).astype(F32), spill, 0.0
+        found = jnp.where(ranks == main_slot, main, 0.0) + jnp.where(
+            ranks == spill_slot, spill, 0.0
         )
         pick_et[first, :] = jnp.sum(found.reshape(BLOCK, ROWS, tokens), axis=1)
-        return carry
-
-    lax.fori_loop(0, count // BLOCK, weigh, 0)
+
+    def take_outs(n, carry):
+        bytes_of(back_outs, group, y_send, y_recv.at[n]).wait_recv()
+        combine(back_outs, n)
+        for b in range(group // BLOCK):
+            weigh(n * (group // BLOCK) + b)
+        return carry
+
+    lax.fori_loop(0, groups, take_outs, 0)
+    moe_out[...] = wide[...].astype(BF16)
     dots = pick_et[...]
     weight_grad = jnp.concatenate(
         [
             jnp.sum(
-                jnp.where(iota((count, tokens), 0) == ids[k : k + 1, :], dots, 0.0),
-                axis=0,
-                keepdims=True,
+                jnp.where(expert_row == ids_t[k : k + 1, :], dots, 0.0), axis=0, keepdims=True
             )
-            for k in range(ids.shape[0])
+            for k in range(ids_t.shape[0])
         ],
         axis=0,
     )
-    score_again = raw[...]
-    sum_again = jnp.sum(score_again, axis=0, keepdims=True)
-    mixing_again = score_again / sum_again
     score_grad[...] = (
-        weight_grad - jnp.sum(mixing_again * weight_grad, axis=0, keepdims=True)
-    ) / sum_again
-
-    parts_wait = bytes_of(pair_in, n_ctx - 1, p_send, p_recv)
-    parts_wait.wait()
-    pair_sum = pair_part[here, :]
-    for j in range(1, n_ctx):
-        pair_sum = pair_sum + pair_in[j]
+        weight_grad - jnp.sum(mixing_t * weight_grad, axis=0, keepdims=True)
+    ) / total_t
+
+    def add_part(distance, total):
+        part_copy(0, distance).wait_recv()
+        return total + pair_in[distance].astype(F32)
+
+    pair_sum = lax.fori_loop(1, n_ctx - ctx, add_part, pair_part[here, :].astype(F32))
     key_grad[...] = pair_sum[:, 0:PAIR].astype(BF16)
     value_grad[...] = pair_sum[:, PAIR:].astype(BF16)
 
     for ref, sem_s, sem_r in (
         (grad_out, g_send, g_recv.at[0]),
         (row_out, x_send, x_recv.at[0]),
-        (row_in, r_send, r_recv),
-        (grad_in, y_send, y_recv),
+        (row_in, r_send, r_recv.at[0]),
+        (grad_in, y_send, y_recv.at[0]),
     ):
         bytes_of(ref, count - 1, sem_s, sem_r).wait_send()
+
+    def sent_pair(peer, carry):
+        for n in range(2):
+            pair_copy(n, peer, ctx).wait_send()
+        return carry
+
+    lax.fori_loop(ctx + 1, n_ctx, sent_pair, 0)
+
+    def sent_part(peer, carry):
+        part_copy(peer, ctx - peer).wait_send()
+        return carry
+
+    lax.fori_loop(0, ctx, sent_part, 0)
+
+
+def settle_kernel(*refs):
+    half = len(refs) // 2
+    copies = [
+        pltpu.make_async_copy(refs[n], refs[half + n], refs[-1].at[n]) for n in range(half)
+    ]
+    for copy in copies:
+        copy.start()
+    for copy in copies:
+        copy.wait()
+
+
+def settle(arrays):
+    hbm = pl.BlockSpec(memory_space=pltpu.HBM)
+    return pl.pallas_call(
+        settle_kernel,
+        out_shape=tuple(jax.ShapeDtypeStruct(a.shape, a.dtype) for a in arrays),
+        in_specs=[hbm] * len(arrays),
+        out_specs=[hbm] * len(arrays),
+        scratch_shapes=[pltpu.SemaphoreType.DMA((len(arrays),))],
+        compiler_params=pltpu.CompilerParams(vmem_limit_bytes=62 * 2**20),
+        name="settle",
+    )(*arrays)
 
 
 def shards(
@@ -626,21 +691,21 @@
             pltpu.VMEM((count, tokens), F32),
             pltpu.VMEM((2, length, PAIR), F32),
             pltpu.VMEM((2, length, PAIR), F32),
-            pltpu.VMEM((length, 2 * PAIR), F32),
-            pltpu.VMEM((n_ctx, tokens, 2 * PAIR), F32),
+            pltpu.VMEM((length, 2 * PAIR), BF16),
+            pltpu.VMEM((n_ctx, tokens, 2 * PAIR), BF16),
             dma((3,)),
-            dma((2,)),
-            dma((2,)),
+            dma((2, n_ctx)),
+            dma((2, n_ctx)),
             dma,
             dma((groups,)),
             dma,
             dma((groups,)),
             dma,
+            dma((groups,)),
             dma,
-            dma,
-            dma,
-            dma,
-            dma,
+            dma((groups,)),
+            dma((n_ctx,)),
+            dma((n_ctx,)),
         ],
         compiler_params=pltpu.CompilerParams(
             collective_id=0, has_side_effects=True, vmem_limit_bytes=63 * 2**20
@@ -657,7 +722,7 @@
         up_weight[0],
         down_weight[0],
     )
-    moe_out, query_grad, key_grad, value_grad, score_grad = outs
+    moe_out, query_grad, key_grad, value_grad, score_grad = settle(outs)
     return (
         moe_out[None],
         query_grad[None],

time: 314 us -> 314 us (level)
  the two profiles are of different devices: /device:TPU:3 before, /device:TPU:0 now
where the time goes in v3:
time: 314 us; the launch traced here: 309 us
  Pallas kernels  309 us (98%)
    pallas_call x1, Pallas kernels, shards(): pl.pallas_call(functools.partial(layer_kernel, n_dp, n_ctx, group), out_s...  274 us
    pallas_call x1, Pallas kernels, settle(): pl.pallas_call(settle_kernel, out_shape=tuple((jax.ShapeDtypeStruct(a.sha...  35 us

profile of v3, /device:TPU:0, one launch (start us, length us, event | category | flops | bytes accessed | tf_op | source)
XLA Modules:
  0.0 309.3 jit_solution(11979281929170622428)
XLA Ops:
  0.6 273.7 %layer.1 = (bf16[128,2048]{1,0:T(8,128)(2,1)}, bf16[128,2048]{1,0:T(8,128)(2,1)}, bf16[128,128]{1,0:T(8,128)(2,1)}, bf16[128,128]{1,0:T(8,128)(2,1)}, f32[8,128]{1,0:T(8,128)}) custom-call(s32[8,128]{1,0:T(8,128)} %bitcast.27, f32[8,128]{1,0:T(8,128)} %bitcast.28, bf16[128,2048]{1,0:T(8,128)(2,1)} %bitcast.23, bf16[128,128]{1,0:T(8,128)(2,1)} %bitcast.25, ...), custom_call_target="tpu_custom_call" | custom-call | tf_op jit(solution)/shard_map/layer/pallas_call | solution.py:654
  274.3 35.0 %settle.1 = (bf16[128,2048]{1,0:T(8,128)(2,1)}, bf16[128,2048]{1,0:T(8,128)(2,1)}, bf16[128,128]{1,0:T(8,128)(2,1)}, bf16[128,128]{1,0:T(8,128)(2,1)}, f32[8,128]{1,0:T(8,128)}) custom-call(bf16[128,2048]{1,0:T(8,128)(2,1)} %get-tuple-element.15.refs_0_, bf16[128,2048]{1,0:T(8,128)(2,1)} %get-tuple-element.16.refs_1_, ...), custom_call_target="tpu_custom_call" | custom-call | tf_op jit(solution)/shard_map/settle/pallas_call | solution.py:616

commit v4 on v3

--- a/solution.py
+++ b/solution.py
@@ -237,7 +237,7 @@
         )
         return dot(to_chunks, stacked).astype(BF16).reshape(BLOCK, ROWS, SPILL)
 
-    def send_out(src, dst, send_sem, recv_sem):
+    def send_out(src, dst, send_sem, recv_sem, held=None):
         def send(step, carry):
             pltpu.make_async_remote_copy(
                 src_ref=src.at[step],
@@ -251,10 +251,14 @@
 
         def body(block, carry):
             pack_block(src, block)
-            lax.fori_loop(jnp.maximum(block * BLOCK, 1), (block + 1) * BLOCK, send, 0)
+            if not held:
+                lax.fori_loop(jnp.maximum(block * BLOCK, 1), (block + 1) * BLOCK, send, 0)
             return carry
 
         lax.fori_loop(0, count // BLOCK, body, 0)
+        if held:
+            held()
+            lax.fori_loop(1, count, send, 0)
         pltpu.make_async_copy(src.at[0], dst.at[0], recv_sem.at[0]).start()
 
     def send_back(src, dst, send_sem, recv_sem, lo, hi):
@@ -367,7 +371,12 @@
     normed = (attn_wide * inv_rms).astype(BF16)
     halves[0:tokens, :] = normed[:, 0:MAIN]
     halves[tokens:, :] = normed[:, MAIN:]
-    send_out(row_out, row_in, x_send, x_recv)
+
+    def grads_here():
+        for n in range(groups):
+            bytes_of(grad_in, group, g_send, g_recv.at[n]).wait_recv()
+
+    send_out(row_out, row_in, x_send, x_recv, grads_here)
 
     scores_t = raw[...]
     total_t = jnp.sum(scores_t, axis=0, keepdims=True)
@@ -429,8 +438,12 @@
 
     def expert(n, carry):
         start = n * group
-        bytes_of(grad_in, group, g_send, g_recv.at[n]).wait_recv()
         bytes_of(row_in, group, x_send, x_recv.at[n]).wait_recv()
+
+        @pl.when(n == groups - 1)
+        def _():
+            send_back(row_in, back_rows, r_send, r_recv, 1, start)
+
         unpack(row_in, start, canon_x)
         unpack(grad_in, start, canon_g)
         gate_act = dot(canon_x[...], w_gate[...])
@@ -443,15 +456,17 @@
         up_grad = (hidden_grad * silu).astype(BF16)
         canon_x[...] = (dot_nt(gate_grad, w_gate[...]) + dot_nt(up_grad, w_up[...])).astype(BF16)
         repack(canon_x, row_in, start)
-        send_back(row_in, back_rows, r_send, r_recv, jnp.maximum(start, 1), start + group)
+
+        @pl.when(n == groups - 1)
+        def _():
+            send_back(row_in, back_rows, r_send, r_recv, jnp.maximum(start, 1), start + group)
+
         canon_g[...] = dot(hidden, w_down[...]).astype(BF16)
         repack(canon_g, grad_in, start)
         return carry
 
     lax.fori_loop(0, groups, expert, 0)
     pltpu.make_async_copy(row_in.at[0], back_rows.at[0], r_recv.at[0]).start()
-    pltpu.make_async_copy(grad_in.at[0], back_outs.at[0], y_recv.at[0]).start()
-    send_back(grad_in, back_outs, y_send, y_recv, 1, count)
 
     def combine(buf, n):
         mine = pl.ds(pl.multiple_of(n * group, group), group)
@@ -476,6 +491,8 @@
         return carry
 
     lax.fori_loop(0, groups, take_rows, 0)
+    pltpu.make_async_copy(grad_in.at[0], back_outs.at[0], y_recv.at[0]).start()
+    send_back(grad_in, back_outs, y_send, y_recv, 1, count)
     normed_grad = wide[...]
     attn_again = attn[...].astype(F32)
     inv = lax.rsqrt(jnp.mean(attn_again * attn_again, axis=1, keepdims=True) + EPSILON)
@@ -601,14 +618,17 @@
 
 
 def settle_kernel(*refs):
-    half = len(refs) // 2
-    copies = [
-        pltpu.make_async_copy(refs[n], refs[half + n], refs[-1].at[n]) for n in range(half)
-    ]
-    for copy in copies:
-        copy.start()
-    for copy in copies:
-        copy.wait()
+    count = (len(refs) - 2) // 3
+    taken, given, held = refs[:count], refs[count : 2 * count], refs[2 * count : 3 * count]
+    loads = [pltpu.make_async_copy(taken[n], held[n], refs[-2].at[n]) for n in range(count)]
+    stores = [pltpu.make_async_copy(held[n], given[n], refs[-1].at[n]) for n in range(count)]
+    for load in loads:
+        load.start()
+    for load, store in zip(loads, stores):
+        load.wait()
+        store.start()
+    for store in stores:
+        store.wait()
 
 
 def settle(arrays):
@@ -618,7 +638,8 @@
         out_shape=tuple(jax.ShapeDtypeStruct(a.shape, a.dtype) for a in arrays),
         in_specs=[hbm] * len(arrays),
         out_specs=[hbm] * len(arrays),
-        scratch_shapes=[pltpu.SemaphoreType.DMA((len(arrays),))],
+        scratch_shapes=[pltpu.VMEM(a.shape, a.dtype) for a in arrays]
+        + [pltpu.SemaphoreType.DMA((len(arrays),))] * 2,
         compiler_params=pltpu.CompilerParams(vmem_limit_bytes=62 * 2**20),
         name="settle",
     )(*arrays)

time: 314 us -> 289 us (0.920); the launches traced: 309 us -> 287 us
  Pallas kernels: 309 us -> 287 us
    pallas_call x1, Pallas kernels: 35 us -> 2.1 us  [settle(): pl.pallas_call(settle_kernel, out_shape=tuple((jax.ShapeDtypeStruct(a.sha...]
    pallas_call x1, Pallas kernels: 274 us -> 285 us  [shards(): pl.pallas_call(functools.partial(layer_kernel, n_dp, n_ctx, group), out_s...]
where the time goes in v4:
time: 289 us; the launch traced here: 287 us
  Pallas kernels  287 us (99%)
    pallas_call x1, Pallas kernels, shards(): pl.pallas_call(functools.partial(layer_kernel, n_dp, n_ctx, group), out_s...  285 us

profile of v4, /device:TPU:0, one launch (start us, length us, event | category | flops | bytes accessed | tf_op | source)
XLA Modules:
  0.0 287.5 jit_solution(3199569464952464684)
XLA Ops:
  0.6 284.7 %layer.1 = (bf16[128,2048]{1,0:T(8,128)(2,1)}, bf16[128,2048]{1,0:T(8,128)(2,1)}, bf16[128,128]{1,0:T(8,128)(2,1)}, bf16[128,128]{1,0:T(8,128)(2,1)}, f32[8,128]{1,0:T(8,128)}) custom-call(s32[8,128]{1,0:T(8,128)} %bitcast.27, f32[8,128]{1,0:T(8,128)} %bitcast.28, bf16[128,2048]{1,0:T(8,128)(2,1)} %bitcast.23, bf16[128,128]{1,0:T(8,128)(2,1)} %bitcast.25, ...), custom_call_target="tpu_custom_call" | custom-call | tf_op jit(solution)/shard_map/layer/pallas_call | solution.py:675
  285.4 2.1 settle.1

commit v5 on v4

--- a/solution.py
+++ b/solution.py
@@ -20,6 +20,7 @@
 CHUNK = MAIN + SPILL
 BLOCK = 16
 PAIR = 128
+HOLD_X, HOLD_R, HOLD_Y = 3, 3, 3
 
 
 def dot(a, b):
@@ -35,11 +36,13 @@
 
 
 def quo(a, n):
-    return lax.shift_right_logical(a, jnp.int32(n.bit_length() - 1)) if a.ndim else a // n
+    if a.ndim:
+        return lax.shift_right_logical(a, jnp.int32(n.bit_length() - 1))
+    return lax.div(a, jnp.int32(n))
 
 
 def rem(a, n):
-    return jnp.bitwise_and(a, n - 1) if a.ndim else a % n
+    return jnp.bitwise_and(a, n - 1) if a.ndim else lax.rem(a, jnp.int32(n))
 
 
 def torus_partner(step, x, y, z, core, sign):
@@ -59,8 +62,8 @@
     dp, ctx = lax.axis_index("dp"), lax.axis_index("ctx")
     count = n_dp * n_ctx
     if (n_dp, n_ctx) == (16, 8):
-        x, core = dp // 4, dp % 2
-        y, z = ctx // 2, (dp // 2) % 2 + 2 * (ctx % 2)
+        x, core = quo(dp, 4), rem(dp, 2)
+        y, z = quo(ctx, 2), rem(quo(dp, 2), 2) + 2 * rem(ctx, 2)
         sign = 1 - 2 * core
 
         def target(step):
@@ -69,7 +72,7 @@
 
         def source(step):
             step = jnp.asarray(step, jnp.int32)
-            other = 1 - 2 * (step // 64)
+            other = 1 - 2 * quo(step, 64)
             return torus_partner(step, x, y, z, core, -sign * other)
 
         return target, source
@@ -81,8 +84,8 @@
         return quo(t, n_ctx), rem(t, n_ctx)
 
     def source(step):
-        t = (me - step + count) % count
-        return t // n_ctx, t % n_ctx
+        t = rem(me - jnp.asarray(step, jnp.int32) + count, count)
+        return quo(t, n_ctx), rem(t, n_ctx)
 
     return target, source
 
@@ -171,7 +174,9 @@
     barrier = pltpu.get_barrier_semaphore()
 
     def greet(step, carry):
-        pl.semaphore_signal(barrier, inc=1, device_id=target(step), device_id_type=MESH)
+        other = rem(me + step, count)
+        where = (quo(other, n_ctx), rem(other, n_ctx))
+        pl.semaphore_signal(barrier, inc=1, device_id=where, device_id_type=MESH)
         return carry
 
     lax.fori_loop(1, count, greet, 0)
@@ -243,7 +248,7 @@
                 src_ref=src.at[step],
                 dst_ref=dst.at[step],
                 send_sem=send_sem,
-                recv_sem=recv_sem.at[step // group],
+                recv_sem=recv_sem.at[quo(step, group)],
                 device_id=target(step),
                 device_id_type=MESH,
             ).start()
@@ -267,7 +272,7 @@
                 src_ref=src.at[step],
                 dst_ref=dst.at[step],
                 send_sem=send_sem,
-                recv_sem=recv_sem.at[step // group],
+                recv_sem=recv_sem.at[quo(step, group)],
                 device_id=source(step),
                 device_id_type=MESH,
             ).start()
@@ -372,8 +377,10 @@
     halves[0:tokens, :] = normed[:, 0:MAIN]
     halves[tokens:, :] = normed[:, MAIN:]
 
+    hold_x, hold_r, hold_y = (min(h, groups) for h in (HOLD_X, HOLD_R, HOLD_Y))
+
     def grads_here():
-        for n in range(groups):
+        for n in range(hold_x):
             bytes_of(grad_in, group, g_send, g_recv.at[n]).wait_recv()
 
     send_out(row_out, row_in, x_send, x_recv, grads_here)
@@ -440,7 +447,11 @@
         start = n * group
         bytes_of(row_in, group, x_send, x_recv.at[n]).wait_recv()
 
-        @pl.when(n == groups - 1)
+        @pl.when(n >= hold_x)
+        def _():
+            bytes_of(grad_in, group, g_send, g_recv.at[n]).wait_recv()
+
+        @pl.when(n == hold_r - 1)
         def _():
             send_back(row_in, back_rows, r_send, r_recv, 1, start)
 
@@ -457,7 +468,7 @@
         canon_x[...] = (dot_nt(gate_grad, w_gate[...]) + dot_nt(up_grad, w_up[...])).astype(BF16)
         repack(canon_x, row_in, start)
 
-        @pl.when(n == groups - 1)
+        @pl.when(n >= hold_r - 1)
         def _():
             send_back(row_in, back_rows, r_send, r_recv, jnp.maximum(start, 1), start + group)
 
@@ -487,12 +498,16 @@
 
     def take_rows(n, carry):
         bytes_of(back_rows, group, r_send, r_recv.at[n]).wait_recv()
+
+        @pl.when(n == hold_y - 1)
+        def _():
+            send_back(grad_in, back_outs, y_send, y_recv, 1, count)
+
         combine(back_rows, n)
         return carry
 
     lax.fori_loop(0, groups, take_rows, 0)
     pltpu.make_async_copy(grad_in.at[0], back_outs.at[0], y_recv.at[0]).start()
-    send_back(grad_in, back_outs, y_send, y_recv, 1, count)
     normed_grad = wide[...]
     attn_again = attn[...].astype(F32)
     inv = lax.rsqrt(jnp.mean(attn_again * attn_again, axis=1, keepdims=True) + EPSILON)

time: 289 us -> 270 us (0.934)
  Pallas kernels: 287 us -> 267 us
    pallas_call x1, Pallas kernels: 285 us -> 265 us  [shards(): pl.pallas_call(functools.partial(layer_kernel, n_dp, n_ctx, group), out_s...]
where the time goes in v5:
time: 270 us; the launch traced here: 267 us
  Pallas kernels  267 us (99%)
    pallas_call x1, Pallas kernels, shards(): pl.pallas_call(functools.partial(layer_kernel, n_dp, n_ctx, group), out_s...  265 us

profile of v5, /device:TPU:0, one launch (start us, length us, event | category | flops | bytes accessed | tf_op | source)
XLA Modules:
  0.0 267.3 jit_solution(9058858571582874494)
XLA Ops:
  0.6 264.6 %layer.1 = (bf16[128,2048]{1,0:T(8,128)(2,1)}, bf16[128,2048]{1,0:T(8,128)(2,1)}, bf16[128,128]{1,0:T(8,128)(2,1)}, bf16[128,128]{1,0:T(8,128)(2,1)}, f32[8,128]{1,0:T(8,128)}) custom-call(s32[8,128]{1,0:T(8,128)} %bitcast.27, f32[8,128]{1,0:T(8,128)} %bitcast.28, bf16[128,2048]{1,0:T(8,128)(2,1)} %bitcast.23, bf16[128,128]{1,0:T(8,128)(2,1)} %bitcast.25, ...), custom_call_target="tpu_custom_call" | custom-call | tf_op jit(solution)/shard_map/layer/pallas_call | solution.py:690
  265.2 2.1 settle.1

commit v6 on v5

--- a/solution.py
+++ b/solution.py
@@ -266,13 +266,13 @@
             lax.fori_loop(1, count, send, 0)
         pltpu.make_async_copy(src.at[0], dst.at[0], recv_sem.at[0]).start()
 
-    def send_back(src, dst, send_sem, recv_sem, lo, hi):
+    def send_back(src, dst, send_sem, recv_sem, lo, hi, size):
         def body(step, carry):
             pltpu.make_async_remote_copy(
                 src_ref=src.at[step],
                 dst_ref=dst.at[step],
                 send_sem=send_sem,
-                recv_sem=recv_sem.at[quo(step, group)],
+                recv_sem=recv_sem.at[quo(step, size)],
                 device_id=source(step),
                 device_id_type=MESH,
             ).start()
@@ -453,7 +453,7 @@
 
         @pl.when(n == hold_r - 1)
         def _():
-            send_back(row_in, back_rows, r_send, r_recv, 1, start)
+            send_back(row_in, back_rows, r_send, r_recv, 1, start, group)
 
         unpack(row_in, start, canon_x)
         unpack(grad_in, start, canon_g)
@@ -470,7 +470,8 @@
 
         @pl.when(n >= hold_r - 1)
         def _():
-            send_back(row_in, back_rows, r_send, r_recv, jnp.maximum(start, 1), start + group)
+            first = jnp.maximum(start, 1)
+            send_back(row_in, back_rows, r_send, r_recv, first, start + group, group)
 
         canon_g[...] = dot(hidden, w_down[...]).astype(BF16)
         repack(canon_g, grad_in, start)
@@ -479,21 +480,23 @@
     lax.fori_loop(0, groups, expert, 0)
     pltpu.make_async_copy(row_in.at[0], back_rows.at[0], r_recv.at[0]).start()
 
-    def combine(buf, n):
-        mine = pl.ds(pl.multiple_of(n * group, group), group)
-        lanes = pl.ds(pl.multiple_of(n * group * ROWS, group * ROWS), group * ROWS)
+    def combine(buf, n, size):
+        mine = pl.ds(pl.multiple_of(n * size, size), size)
+        lanes = pl.ds(pl.multiple_of(n * size * ROWS, size * ROWS), size * ROWS)
         for c in range(4):
-            rows = buf[mine, :, c * 256 : (c + 1) * 256].reshape(group * ROWS, 256)
+            rows = buf[mine, :, c * 256 : (c + 1) * 256].reshape(size * ROWS, 256)
             part = dot(mix_main[:, lanes], rows)
             wide[:, c * 256 : (c + 1) * 256] += part[0:tokens]
             wide[:, MAIN + c * 256 : MAIN + (c + 1) * 256] += part[tokens:]
-        spill = buf[mine, :, MAIN:].reshape(group * ROWS, SPILL)
+        spill = buf[mine, :, MAIN:].reshape(size * ROWS, SPILL)
         spill_mix = mix_spill[:, lanes].astype(F32)
-        column_block = quo(rem(iota((tokens, group * ROWS), 1), ROWS), 2)
+        column_block = quo(rem(iota((tokens, size * ROWS), 1), ROWS), 2)
         for c in range(8):
             picked = jnp.where(column_block == c, spill_mix, 0.0).astype(BF16)
             wide[:, c * SPILL : (c + 1) * SPILL] += dot(picked, spill)
 
+    late = max(1, count - BLOCK)
+
     wide[...] = jnp.zeros_like(wide)
 
     def take_rows(n, carry):
@@ -501,9 +504,9 @@
 
         @pl.when(n == hold_y - 1)
         def _():
-            send_back(grad_in, back_outs, y_send, y_recv, 1, count)
-
-        combine(back_rows, n)
+            send_back(grad_in, back_outs, y_send, y_recv, 1, late, BLOCK)
+
+        combine(back_rows, n, group)
         return carry
 
     lax.fori_loop(0, groups, take_rows, 0)
@@ -563,6 +566,7 @@
         return carry
 
     lax.fori_loop(0, ctx, send_part, 0)
+    send_back(grad_in, back_outs, y_send, y_recv, late, count, BLOCK)
 
     wide[...] = jnp.zeros_like(wide)
 
@@ -580,13 +584,12 @@
         pick_et[first, :] = jnp.sum(found.reshape(BLOCK, ROWS, tokens), axis=1)
 
     def take_outs(n, carry):
-        bytes_of(back_outs, group, y_send, y_recv.at[n]).wait_recv()
-        combine(back_outs, n)
-        for b in range(group // BLOCK):
-            weigh(n * (group // BLOCK) + b)
-        return carry
-
-    lax.fori_loop(0, groups, take_outs, 0)
+        bytes_of(back_outs, BLOCK, y_send, y_recv.at[n]).wait_recv()
+        combine(back_outs, n, BLOCK)
+        weigh(n)
+        return carry
+
+    lax.fori_loop(0, count // BLOCK, take_outs, 0)
     moe_out[...] = wide[...].astype(BF16)
     dots = pick_et[...]
     weight_grad = jnp.concatenate(
@@ -739,7 +742,7 @@
             dma,
             dma((groups,)),
             dma,
-            dma((groups,)),
+            dma((count // BLOCK,)),
             dma((n_ctx,)),
             dma((n_ctx,)),
         ],

time: 270 us -> 271 us (level)
  no operation moved by 1% of the time
where the time goes in v6:
time: 271 us; the launch traced here: 268 us
  Pallas kernels  267 us (99%)
    pallas_call x1, Pallas kernels, shards(): pl.pallas_call(functools.partial(layer_kernel, n_dp, n_ctx, group), out_s...  265 us

profile of v6, /device:TPU:0, one launch (start us, length us, event | category | flops | bytes accessed | tf_op | source)
XLA Modules:
  0.0 267.8 jit_solution(7624297790818855922)
XLA Ops:
  0.6 265.0 %layer.1 = (bf16[128,2048]{1,0:T(8,128)(2,1)}, bf16[128,2048]{1,0:T(8,128)(2,1)}, bf16[128,128]{1,0:T(8,128)(2,1)}, bf16[128,128]{1,0:T(8,128)(2,1)}, f32[8,128]{1,0:T(8,128)}) custom-call(s32[8,128]{1,0:T(8,128)} %bitcast.27, f32[8,128]{1,0:T(8,128)} %bitcast.28, bf16[128,2048]{1,0:T(8,128)(2,1)} %bitcast.23, bf16[128,128]{1,0:T(8,128)(2,1)} %bitcast.25, ...), custom_call_target="tpu_custom_call" | custom-call | tf_op jit(solution)/shard_map/layer/pallas_call | solution.py:693
  265.7 2.1 settle.1

commit v7 on v5

--- a/solution.py
+++ b/solution.py
@@ -255,8 +255,10 @@
             return carry
 
         def body(block, carry):
-            pack_block(src, block)
-            if not held:
+            if held:
+                pack_block(src, block)
+            else:
+                pl.when(block > 0)(lambda: pack_block(src, block))
                 lax.fori_loop(jnp.maximum(block * BLOCK, 1), (block + 1) * BLOCK, send, 0)
             return carry
 
@@ -291,6 +293,9 @@
             device_id_type=MESH,
         )
 
+    halves[0:tokens, :] = out_grad[:, 0:MAIN]
+    halves[tokens:, :] = out_grad[:, MAIN:]
+    pack_block(grad_out, 0)
     pl.semaphore_wait(barrier, count - 1)
     here = pl.ds(pl.multiple_of(ctx * tokens, tokens), tokens)
     pair_copies = ((keys, all_keys), (values, all_values))
@@ -311,8 +316,6 @@
         return carry
 
     lax.fori_loop(ctx + 1, n_ctx, send_pair, 0)
-    halves[0:tokens, :] = out_grad[:, 0:MAIN]
-    halves[tokens:, :] = out_grad[:, MAIN:]
     send_out(grad_out, grad_in, g_send, g_recv)
     for copy in weight_copies:
         copy.start()

time: 270 us -> 286 us (1.059); the launches traced: 267 us -> 286 us
  Pallas kernels: 267 us -> 286 us
    pallas_call x1, Pallas kernels: 265 us -> 284 us  [shards(): pl.pallas_call(functools.partial(layer_kernel, n_dp, n_ctx, group), out_s...]
where the time goes in v7:
time: 286 us
  Pallas kernels  286 us (100%)
    pallas_call x1, Pallas kernels, shards(): pl.pallas_call(functools.partial(layer_kernel, n_dp, n_ctx, group), out_s...  284 us

profile of v7, /device:TPU:0, one launch (start us, length us, event | category | flops | bytes accessed | tf_op | source)
XLA Modules:
  0.0 286.2 jit_solution(3823108837823705683)
XLA Ops:
  0.6 283.5 %layer.1 = (bf16[128,2048]{1,0:T(8,128)(2,1)}, bf16[128,2048]{1,0:T(8,128)(2,1)}, bf16[128,128]{1,0:T(8,128)(2,1)}, bf16[128,128]{1,0:T(8,128)(2,1)}, f32[8,128]{1,0:T(8,128)}) custom-call(s32[8,128]{1,0:T(8,128)} %bitcast.27, f32[8,128]{1,0:T(8,128)} %bitcast.28, bf16[128,2048]{1,0:T(8,128)(2,1)} %bitcast.23, bf16[128,128]{1,0:T(8,128)(2,1)} %bitcast.25, ...), custom_call_target="tpu_custom_call" | custom-call | tf_op jit(solution)/shard_map/layer/pallas_call | solution.py:693
  284.1 2.1 settle.1
